TPU v7x, 512 devices: a whole 4x4x16 slice. The times are simulated.
512 devices in a mesh: leaf: 512 (over y, z, x, core).
Axes of the slice: x: 4, y: 4, z: 16, core: 2. Of those that a mesh axis runs over, the one named last changes fastest.
Arguments:
- rhs: bfloat16 [4, 16384], P(None, 'leaf'), may hold values from -6 to 6
- x_sep: bfloat16 [16384, 29400], P('leaf'), may hold values from -2 to 2
- x_loc: bfloat16 [16384, 4096], P('leaf'), may hold values from -2 to 2
- sep_sizes: int32 [9], replicated, may hold values from 100 to 12800, as said below
Outputs:
- solution: float32 [4, 16384], P(None, 'leaf')
Inputs may be any that keep to these rules, and one draw needn't show every extreme that they name: `sep_sizes`: entry l counts the active leading columns of level l, from half of its width 12800 // (4^(l // 3) * 2^(l % 3)), rounded down, to all of it; entry 0 is always complete and the last entry always holds exactly half of its width.
All inputs are finite; a program needn't handle non-finite values.
Results may differ from a plain program's by a relative error of at most 0.0004.
Values may be sent and summed in bfloat16 or wider, within the bound.
A program may use at most 64 MiB of HBM per device.

v0:
```python
import jax
import jax.numpy as jnp
from jax import lax
from jax.sharding import PartitionSpec as P

SEP_TOP = 12800


def from_behind(value, axis, steps):
    count = lax.axis_size(axis)
    first, last = (max(0, -steps), min(count, count - steps))
    return lax.ppermute(value, axis, [(source, source + steps) for source in range(first, last)])


def level_width(top, level_no):
    return top // (4 ** (level_no // 3) * 2 ** (level_no % 3))


def contract_columns(left, right):
    return lax.dot_general(
        left, right, (((1,), (1,)), ((), ())), preferred_element_type=jnp.float32
    )


def mask_round(values, limit):
    columns = jnp.arange(values.shape[1], dtype=jnp.int32)
    return jnp.where((columns < limit)[None, :], values, jnp.float32(0.0)).astype(jnp.bfloat16)


def mask_levels(values, widths, sep_sizes, first_level):
    pieces = []
    cursor = 0
    for level_no in range(first_level, len(widths)):
        span = widths[level_no]
        pieces.append(mask_round(values[:, cursor : cursor + span], sep_sizes[level_no]))
        cursor = cursor + span
    return jnp.concatenate(pieces, axis=1)


def body(rhs, x_sep, x_loc, sep_sizes):
    levels = lax.axis_size("leaf").bit_length() - 1
    widths = [level_width(SEP_TOP, level_no) for level_no in range(levels)]
    level_ends = [sum(widths[: level_no + 1]) for level_no in range(levels)]
    position = lax.axis_index("leaf")
    contrib = jnp.dot(rhs, x_sep, preferred_element_type=jnp.float32)
    skip_top = 0
    lower_start = widths[0] * skip_top
    lower_sums = contrib
    interior = jnp.dot(rhs, x_loc, preferred_element_type=jnp.float32).astype(jnp.bfloat16)
    for bit_index in range(levels - skip_top):
        column_end = level_ends[levels - 1 - bit_index] - lower_start
        arrived = from_behind(lower_sums[:, :column_end], "leaf", -(1 << bit_index))
        lower_sums = jnp.concatenate(
            [lower_sums[:, :column_end] + arrived, lower_sums[:, column_end:]], axis=1
        )
    lower_coarse = mask_levels(lower_sums, widths, sep_sizes, skip_top)
    for bit_index in reversed(range(levels - skip_top)):
        column_end = level_ends[levels - 1 - bit_index] - lower_start
        arrived = from_behind(lower_coarse[:, :column_end], "leaf", 1 << bit_index)
        receives = jnp.bitwise_and(jnp.right_shift(position, bit_index), 1) == 1
        lower_coarse = jnp.concatenate(
            [
                jnp.where(receives, arrived, lower_coarse[:, :column_end]),
                lower_coarse[:, column_end:],
            ],
            axis=1,
        )
    return contract_columns(lower_coarse, x_sep) + contract_columns(interior, x_loc)


def solution(mesh):
    placed = (P(None, "leaf"), P("leaf", None), P("leaf", None), P())
    return jax.shard_map(
        body, mesh=mesh, in_specs=placed, out_specs=P(None, "leaf"), check_vma=False
    )
```

profile of v0, /device:TPU:16, one launch (start us, length us, event | category | flops | bytes accessed | tf_op | source)
XLA Modules:
  0.0 305.3 jit_solution(14970160502727613290)
XLA Ops:
  2.6 12.9 %collective-permute-start = (f32[4,29400]{1,0:T(4,128)S(1)}, f32[4,29400]{1,0:T(4,128)S(1)}, u32[]{:S(2)}, u32[]{:S(2)}) collective-permute-start(f32[4,29400]{1,0:T(4,128)S(1)} %fusion.12), channel_id=1, source_target_pairs={{1,0},{2,1},{3,2},{4,3},{5,4},{6,5},{7,6},{8,7},{9,8},{10,9},{11,1... | collective-permute-start | bytes 1411208 | tf_op jit(solution)/shard_map/ppermute | solution.py:12
  15.5 6.1 %collective-permute-done = f32[4,29400]{1,0:T(4,128)S(1)} collective-permute-done((f32[4,29400]{1,0:T(4,128)S(1)}, f32[4,29400]{1,0:T(4,128)S(1)}, u32[]{:S(2)}, u32[]{:S(2)}) %collective-permute-start) | collective-permute-done | bytes 470432 | tf_op jit(solution)/shard_map/ppermute | solution.py:12
  21.8 2.7 collective-permute-start.1
  24.5 7.7 %collective-permute-done.1 = f32[4,29200]{1,0:T(4,128)S(1)} collective-permute-done((f32[4,29200]{1,0:T(4,128)S(1)}, f32[4,29200]{1,0:T(4,128)S(1)}, u32[]{:S(2)}, u32[]{:S(2)}) %collective-permute-start.1) | collective-permute-done | bytes 467232 | tf_op jit(solution)/shard_map/ppermute | solution.py:12
  32.4 5.1 %collective-permute-start.2 = (f32[4,28800]{1,0:T(4,128)S(1)}, f32[4,28800]{1,0:T(4,128)S(1)}, u32[]{:S(2)}, u32[]{:S(2)}) collective-permute-start(f32[4,28800]{1,0:T(4,128)S(1)} %slice.220), channel_id=1, source_target_pairs={{4,0},{5,1},{6,2},{7,3},{8,4},{9,5},{10,6},{11,7},{12,8},{13,9},{1... | collective-permute-start | bytes 1382408 | tf_op jit(solution)/shard_map/ppermute | solution.py:12
  37.5 9.3 %collective-permute-done.2 = f32[4,28800]{1,0:T(4,128)S(1)} collective-permute-done((f32[4,28800]{1,0:T(4,128)S(1)}, f32[4,28800]{1,0:T(4,128)S(1)}, u32[]{:S(2)}, u32[]{:S(2)}) %collective-permute-start.2) | collective-permute-done | bytes 460832 | tf_op jit(solution)/shard_map/ppermute | solution.py:12
  46.9 7.9 %collective-permute-start.3 = (f32[4,28000]{1,0:T(4,128)S(1)}, f32[4,28000]{1,0:T(4,128)S(1)}, u32[]{:S(2)}, u32[]{:S(2)}) collective-permute-start(f32[4,28000]{1,0:T(4,128)S(1)} %slice.221), channel_id=1, source_target_pairs={{8,0},{9,1},{10,2},{11,3},{12,4},{13,5},{14,6},{15,7},{16,8},{17,9... | collective-permute-start | bytes 1344008 | tf_op jit(solution)/shard_map/ppermute | solution.py:12
  54.9 9.2 %collective-permute-done.3 = f32[4,28000]{1,0:T(4,128)S(1)} collective-permute-done((f32[4,28000]{1,0:T(4,128)S(1)}, f32[4,28000]{1,0:T(4,128)S(1)}, u32[]{:S(2)}, u32[]{:S(2)}) %collective-permute-start.3) | collective-permute-done | bytes 448032 | tf_op jit(solution)/shard_map/ppermute | solution.py:12
  64.2 5.0 %collective-permute-start.4 = (f32[4,27200]{1,0:T(4,128)S(1)}, f32[4,27200]{1,0:T(4,128)S(1)}, u32[]{:S(2)}, u32[]{:S(2)}) collective-permute-start(f32[4,27200]{1,0:T(4,128)S(1)} %slice.222), channel_id=1, source_target_pairs={{16,0},{17,1},{18,2},{19,3},{20,4},{21,5},{22,6},{23,7},{24,8},{25... | collective-permute-start | bytes 1305608 | tf_op jit(solution)/shard_map/ppermute | solution.py:12
  69.2 17.8 %collective-permute-done.4 = f32[4,27200]{1,0:T(4,128)S(1)} collective-permute-done((f32[4,27200]{1,0:T(4,128)S(1)}, f32[4,27200]{1,0:T(4,128)S(1)}, u32[]{:S(2)}, u32[]{:S(2)}) %collective-permute-start.4) | collective-permute-done | bytes 435232 | tf_op jit(solution)/shard_map/ppermute | solution.py:12
  87.2 5.6 %collective-permute-start.5 = (f32[4,25600]{1,0:T(4,128)S(1)}, f32[4,25600]{1,0:T(4,128)S(1)}, u32[]{:S(2)}, u32[]{:S(2)}) collective-permute-start(f32[4,25600]{1,0:T(4,128)S(1)} %slice.223), channel_id=1, source_target_pairs={{32,0},{33,1},{34,2},{35,3},{36,4},{37,5},{38,6},{39,7},{40,8},{41... | collective-permute-start | bytes 1228808 | tf_op jit(solution)/shard_map/ppermute | solution.py:12
  92.8 48.4 %collective-permute-done.5 = f32[4,25600]{1,0:T(4,128)S(1)} collective-permute-done((f32[4,25600]{1,0:T(4,128)S(1)}, f32[4,25600]{1,0:T(4,128)S(1)}, u32[]{:S(2)}, u32[]{:S(2)}) %collective-permute-start.5) | collective-permute-done | bytes 409632 | tf_op jit(solution)/shard_map/ppermute | solution.py:12
  146.6 18.5 %collective-permute-done.6 = f32[4,22400]{1,0:T(4,128)} collective-permute-done((f32[4,22400]{1,0:T(4,128)}, f32[4,22400]{1,0:T(4,128)}, u32[]{:S(2)}, u32[]{:S(2)}) %collective-permute-start.6) | collective-permute-done | bytes 358432 | tf_op jit(solution)/shard_map/ppermute | solution.py:12
  166.4 1.9 collective-permute-start.7
  170.3 6.1 %collective-permute-done.7 = f32[4,19200]{1,0:T(4,128)S(1)} collective-permute-done((f32[4,19200]{1,0:T(4,128)S(1)}, f32[4,19200]{1,0:T(4,128)S(1)}, u32[]{:S(2)}, u32[]{:S(2)}) %collective-permute-start.7) | collective-permute-done | bytes 307232 | tf_op jit(solution)/shard_map/ppermute | solution.py:12
  178.7 2.6 collective-permute-done.8
  182.7 6.7 %collective-permute-done.9 = bf16[4,12800]{1,0:T(4,128)(2,1)S(1)} collective-permute-done((bf16[4,12800]{1,0:T(4,128)(2,1)S(1)}, bf16[4,12800]{1,0:T(4,128)(2,1)S(1)}, u32[]{:S(2)}, u32[]{:S(2)}) %collective-permute-start.9) | collective-permute-done | bytes 102432 | tf_op jit(solution)/shard_map/ppermute | solution.py:12
  189.5 4.7 %collective-permute-start.10 = (bf16[4,19200]{1,0:T(4,128)(2,1)S(1)}, bf16[4,19200]{1,0:T(4,128)(2,1)S(1)}, u32[]{:S(2)}, u32[]{:S(2)}) collective-permute-start(bf16[4,19200]{1,0:T(4,128)(2,1)S(1)} %pad_maximum_fusion.7), channel_id=1, source_target_pairs={{0,128},{1,129},{2,130},{3,131},{4,132},{5,133},{6,134},{7,135},{8... | collective-permute-start | bytes 460808 | tf_op jit(solution)/shard_map/ppermute | solution.py:12
  194.3 2.7 collective-permute-done.10
  197.1 8.0 %collective-permute-start.11 = (bf16[4,22400]{1,0:T(4,128)(2,1)S(1)}, bf16[4,22400]{1,0:T(4,128)(2,1)S(1)}, u32[]{:S(2)}, u32[]{:S(2)}) collective-permute-start(bf16[4,22400]{1,0:T(4,128)(2,1)S(1)} %pad_maximum_fusion.6), channel_id=1, source_target_pairs={{0,64},{1,65},{2,66},{3,67},{4,68},{5,69},{6,70},{7,71},{8,72},{9,... | collective-permute-start | bytes 537608 | tf_op jit(solution)/shard_map/ppermute | solution.py:12
  206.0 8.3 %collective-permute-done.11 = bf16[4,22400]{1,0:T(4,128)(2,1)S(1)} collective-permute-done((bf16[4,22400]{1,0:T(4,128)(2,1)S(1)}, bf16[4,22400]{1,0:T(4,128)(2,1)S(1)}, u32[]{:S(2)}, u32[]{:S(2)}) %collective-permute-start.11) | collective-permute-done | bytes 179232 | tf_op jit(solution)/shard_map/ppermute | solution.py:12
  214.4 3.8 %collective-permute-start.12 = (bf16[4,25600]{1,0:T(4,128)(2,1)S(1)}, bf16[4,25600]{1,0:T(4,128)(2,1)S(1)}, u32[]{:S(2)}, u32[]{:S(2)}) collective-permute-start(bf16[4,25600]{1,0:T(4,128)(2,1)S(1)} %pad_maximum_fusion.5), channel_id=1, source_target_pairs={{0,32},{1,33},{2,34},{3,35},{4,36},{5,37},{6,38},{7,39},{8,40},{9,... | collective-permute-start | bytes 614408 | tf_op jit(solution)/shard_map/ppermute | solution.py:12
  219.0 8.0 %collective-permute-done.12 = bf16[4,25600]{1,0:T(4,128)(2,1)S(1)} collective-permute-done((bf16[4,25600]{1,0:T(4,128)(2,1)S(1)}, bf16[4,25600]{1,0:T(4,128)(2,1)S(1)}, u32[]{:S(2)}, u32[]{:S(2)}) %collective-permute-start.12) | collective-permute-done | bytes 204832 | tf_op jit(solution)/shard_map/ppermute | solution.py:12
  227.2 24.7 %collective-permute-start.13 = (bf16[4,27200]{1,0:T(4,128)(2,1)S(1)}, bf16[4,27200]{1,0:T(4,128)(2,1)S(1)}, u32[]{:S(2)}, u32[]{:S(2)}) collective-permute-start(bf16[4,27200]{1,0:T(4,128)(2,1)S(1)} %pad_maximum_fusion.4), channel_id=1, source_target_pairs={{0,16},{1,17},{2,18},{3,19},{4,20},{5,21},{6,22},{7,23},{8,24},{9,... | collective-permute-start | bytes 652808 | tf_op jit(solution)/shard_map/ppermute | solution.py:12
  252.8 3.2 %collective-permute-done.13 = bf16[4,27200]{1,0:T(4,128)(2,1)S(1)} collective-permute-done((bf16[4,27200]{1,0:T(4,128)(2,1)S(1)}, bf16[4,27200]{1,0:T(4,128)(2,1)S(1)}, u32[]{:S(2)}, u32[]{:S(2)}) %collective-permute-start.13) | collective-permute-done | bytes 217632 | tf_op jit(solution)/shard_map/ppermute | solution.py:12
  256.2 1.9 collective-permute-start.14
  258.2 8.0 %collective-permute-done.14 = bf16[4,28000]{1,0:T(4,128)(2,1)S(1)} collective-permute-done((bf16[4,28000]{1,0:T(4,128)(2,1)S(1)}, bf16[4,28000]{1,0:T(4,128)(2,1)S(1)}, u32[]{:S(2)}, u32[]{:S(2)}) %collective-permute-start.14) | collective-permute-done | bytes 224032 | tf_op jit(solution)/shard_map/ppermute | solution.py:12
  266.5 4.4 %collective-permute-start.15 = (bf16[4,28800]{1,0:T(4,128)(2,1)S(1)}, bf16[4,28800]{1,0:T(4,128)(2,1)}, u32[]{:S(2)}, u32[]{:S(2)}) collective-permute-start(bf16[4,28800]{1,0:T(4,128)(2,1)S(1)} %pad_maximum_fusion.2), channel_id=1, source_target_pairs={{0,4},{1,5},{2,6},{3,7},{4,8},{5,9},{6,10},{7,11},{8,12},{9,13},{1... | collective-permute-start | bytes 691208 | tf_op jit(solution)/shard_map/ppermute | solution.py:12
  272.7 6.3 %collective-permute-done.15 = bf16[4,28800]{1,0:T(4,128)(2,1)} collective-permute-done((bf16[4,28800]{1,0:T(4,128)(2,1)S(1)}, bf16[4,28800]{1,0:T(4,128)(2,1)}, u32[]{:S(2)}, u32[]{:S(2)}) %collective-permute-start.15) | collective-permute-done | bytes 230432 | tf_op jit(solution)/shard_map/ppermute | solution.py:12
  280.0 2.6 collective-permute-start.16
  283.3 8.9 %collective-permute-done.16 = bf16[4,29200]{1,0:T(4,128)(2,1)S(1)} collective-permute-done((bf16[4,29200]{1,0:T(4,128)(2,1)S(1)}, bf16[4,29200]{1,0:T(4,128)(2,1)S(1)}, u32[]{:S(2)}, u32[]{:S(2)}) %collective-permute-start.16) | collective-permute-done | bytes 233632 | tf_op jit(solution)/shard_map/ppermute | solution.py:12
  294.7 9.4 %collective-permute-done.17 = bf16[4,29400]{1,0:T(4,128)(2,1)S(1)} collective-permute-done((bf16[4,29400]{1,0:T(4,128)(2,1)S(1)}, bf16[4,29400]{1,0:T(4,128)(2,1)S(1)}, u32[]{:S(2)}, u32[]{:S(2)}) %collective-permute-start.17) | collective-permute-done | bytes 235232 | tf_op jit(solution)/shard_map/ppermute | solution.py:12
  (74 shorter events, 26.5 us)
Async XLA Ops:
  0.0 1.5 copy-start
  2.6 19.0 %collective-permute-start = (f32[4,29400]{1,0:T(4,128)S(1)}, f32[4,29400]{1,0:T(4,128)S(1)}, u32[]{:S(2)}, u32[]{:S(2)}) collective-permute-start(f32[4,29400]{1,0:T(4,128)S(1)} %fusion.12), channel_id=1, source_target_pairs={{1,0},{2,1},{3,2},{4,3},{5,4},{6,5},{7,6},{8,7},{9,8},{10,9},{11,1... | collective-permute-start | bytes 1411208 | tf_op jit(solution)/shard_map/ppermute | solution.py:12
  21.8 10.5 %collective-permute-start.1 = (f32[4,29200]{1,0:T(4,128)S(1)}, f32[4,29200]{1,0:T(4,128)S(1)}, u32[]{:S(2)}, u32[]{:S(2)}) collective-permute-start(f32[4,29200]{1,0:T(4,128)S(1)} %slice.219), channel_id=1, source_target_pairs={{2,0},{3,1},{4,2},{5,3},{6,4},{7,5},{8,6},{9,7},{10,8},{11,9},{12,... | collective-permute-start | bytes 1401608 | tf_op jit(solution)/shard_map/ppermute | solution.py:12
  32.4 14.4 %collective-permute-start.2 = (f32[4,28800]{1,0:T(4,128)S(1)}, f32[4,28800]{1,0:T(4,128)S(1)}, u32[]{:S(2)}, u32[]{:S(2)}) collective-permute-start(f32[4,28800]{1,0:T(4,128)S(1)} %slice.220), channel_id=1, source_target_pairs={{4,0},{5,1},{6,2},{7,3},{8,4},{9,5},{10,6},{11,7},{12,8},{13,9},{1... | collective-permute-start | bytes 1382408 | tf_op jit(solution)/shard_map/ppermute | solution.py:12
  46.9 17.1 %collective-permute-start.3 = (f32[4,28000]{1,0:T(4,128)S(1)}, f32[4,28000]{1,0:T(4,128)S(1)}, u32[]{:S(2)}, u32[]{:S(2)}) collective-permute-start(f32[4,28000]{1,0:T(4,128)S(1)} %slice.221), channel_id=1, source_target_pairs={{8,0},{9,1},{10,2},{11,3},{12,4},{13,5},{14,6},{15,7},{16,8},{17,9... | collective-permute-start | bytes 1344008 | tf_op jit(solution)/shard_map/ppermute | solution.py:12
  64.2 77.2 %copy-start.1 = (f32[4,28000]{1,0:T(4,128)}, f32[4,28000]{1,0:T(4,128)S(1)}, u32[]{:S(2)}) copy-start(f32[4,28000]{1,0:T(4,128)S(1)} %slice_add_fusion.4) | copy-start | bytes 1344004
  64.2 79.9 %copy-start.6 = (s32[9]{0:T(128)S(1)}, s32[9]{0:T(128)}, u32[]{:S(2)}) copy-start(s32[9]{0:T(128)} %param.7) | copy-start | bytes 112
  64.2 22.8 %collective-permute-start.4 = (f32[4,27200]{1,0:T(4,128)S(1)}, f32[4,27200]{1,0:T(4,128)S(1)}, u32[]{:S(2)}, u32[]{:S(2)}) collective-permute-start(f32[4,27200]{1,0:T(4,128)S(1)} %slice.222), channel_id=1, source_target_pairs={{16,0},{17,1},{18,2},{19,3},{20,4},{21,5},{22,6},{23,7},{24,8},{25... | collective-permute-start | bytes 1305608 | tf_op jit(solution)/shard_map/ppermute | solution.py:12
  87.2 55.0 %copy-start.2 = (f32[4,27200]{1,0:T(4,128)}, f32[4,27200]{1,0:T(4,128)S(1)}, u32[]{:S(2)}) copy-start(f32[4,27200]{1,0:T(4,128)S(1)} %slice_add_fusion.3) | copy-start | bytes 1305604
  87.2 54.0 %collective-permute-start.5 = (f32[4,25600]{1,0:T(4,128)S(1)}, f32[4,25600]{1,0:T(4,128)S(1)}, u32[]{:S(2)}, u32[]{:S(2)}) collective-permute-start(f32[4,25600]{1,0:T(4,128)S(1)} %slice.223), channel_id=1, source_target_pairs={{32,0},{33,1},{34,2},{35,3},{36,4},{37,5},{38,6},{39,7},{40,8},{41... | collective-permute-start | bytes 1228808 | tf_op jit(solution)/shard_map/ppermute | solution.py:12
  141.3 2.8 copy-start.3
  142.2 23.0 %collective-permute-start.6 = (f32[4,22400]{1,0:T(4,128)}, f32[4,22400]{1,0:T(4,128)}, u32[]{:S(2)}, u32[]{:S(2)}) collective-permute-start(f32[4,22400]{1,0:T(4,128)} %slice.224), channel_id=1, source_target_pairs={{64,0},{65,1},{66,2},{67,3},{68,4},{69,5},{70,6},{71,7},{72,8},{73... | collective-permute-start | bytes 1075208 | tf_op jit(solution)/shard_map/ppermute | solution.py:12
  166.4 10.0 %collective-permute-start.7 = (f32[4,19200]{1,0:T(4,128)S(1)}, f32[4,19200]{1,0:T(4,128)S(1)}, u32[]{:S(2)}, u32[]{:S(2)}) collective-permute-start(f32[4,19200]{1,0:T(4,128)S(1)} %slice.225), channel_id=1, source_target_pairs={{128,0},{129,1},{130,2},{131,3},{132,4},{133,5},{134,6},{135,7},{1... | collective-permute-start | bytes 921608 | tf_op jit(solution)/shard_map/ppermute | solution.py:12
  176.5 4.7 %collective-permute-start.8 = (f32[4,12800]{1,0:T(4,128)S(1)}, f32[4,12800]{1,0:T(4,128)S(1)}, u32[]{:S(2)}, u32[]{:S(2)}) collective-permute-start(f32[4,12800]{1,0:T(4,128)S(1)} %slice.226), channel_id=1, source_target_pairs={{256,0},{257,1},{258,2},{259,3},{260,4},{261,5},{262,6},{263,7},{2... | collective-permute-start | bytes 614408 | tf_op jit(solution)/shard_map/ppermute | solution.py:12
  181.3 8.1 %collective-permute-start.9 = (bf16[4,12800]{1,0:T(4,128)(2,1)S(1)}, bf16[4,12800]{1,0:T(4,128)(2,1)S(1)}, u32[]{:S(2)}, u32[]{:S(2)}) collective-permute-start(bf16[4,12800]{1,0:T(4,128)(2,1)S(1)} %select_convert_fusion), channel_id=1, source_target_pairs={{0,256},{1,257},{2,258},{3,259},{4,260},{5,261},{6,262},{7,263},{8... | collective-permute-start | bytes 307208 | tf_op jit(solution)/shard_map/ppermute | solution.py:12
  189.5 7.4 %collective-permute-start.10 = (bf16[4,19200]{1,0:T(4,128)(2,1)S(1)}, bf16[4,19200]{1,0:T(4,128)(2,1)S(1)}, u32[]{:S(2)}, u32[]{:S(2)}) collective-permute-start(bf16[4,19200]{1,0:T(4,128)(2,1)S(1)} %pad_maximum_fusion.7), channel_id=1, source_target_pairs={{0,128},{1,129},{2,130},{3,131},{4,132},{5,133},{6,134},{7,135},{8... | collective-permute-start | bytes 460808 | tf_op jit(solution)/shard_map/ppermute | solution.py:12
  197.1 17.1 %collective-permute-start.11 = (bf16[4,22400]{1,0:T(4,128)(2,1)S(1)}, bf16[4,22400]{1,0:T(4,128)(2,1)S(1)}, u32[]{:S(2)}, u32[]{:S(2)}) collective-permute-start(bf16[4,22400]{1,0:T(4,128)(2,1)S(1)} %pad_maximum_fusion.6), channel_id=1, source_target_pairs={{0,64},{1,65},{2,66},{3,67},{4,68},{5,69},{6,70},{7,71},{8,72},{9,... | collective-permute-start | bytes 537608 | tf_op jit(solution)/shard_map/ppermute | solution.py:12
  214.4 12.6 %collective-permute-start.12 = (bf16[4,25600]{1,0:T(4,128)(2,1)S(1)}, bf16[4,25600]{1,0:T(4,128)(2,1)S(1)}, u32[]{:S(2)}, u32[]{:S(2)}) collective-permute-start(bf16[4,25600]{1,0:T(4,128)(2,1)S(1)} %pad_maximum_fusion.5), channel_id=1, source_target_pairs={{0,32},{1,33},{2,34},{3,35},{4,36},{5,37},{6,38},{7,39},{8,40},{9,... | collective-permute-start | bytes 614408 | tf_op jit(solution)/shard_map/ppermute | solution.py:12
  227.2 28.7 %collective-permute-start.13 = (bf16[4,27200]{1,0:T(4,128)(2,1)S(1)}, bf16[4,27200]{1,0:T(4,128)(2,1)S(1)}, u32[]{:S(2)}, u32[]{:S(2)}) collective-permute-start(bf16[4,27200]{1,0:T(4,128)(2,1)S(1)} %pad_maximum_fusion.4), channel_id=1, source_target_pairs={{0,16},{1,17},{2,18},{3,19},{4,20},{5,21},{6,22},{7,23},{8,24},{9,... | collective-permute-start | bytes 652808 | tf_op jit(solution)/shard_map/ppermute | solution.py:12
  256.1 38.4 %copy-start.4 = (bf16[32,4096]{1,0:T(8,128)(2,1)S(1)}, bf16[32,4096]{1,0:T(8,128)(2,1)}, u32[]{:S(2)}) copy-start(bf16[32,4096]{1,0:T(8,128)(2,1)} %param.6) | copy-start | bytes 786436
  256.1 38.4 %copy-start.7 = (bf16[4,32]{1,0:T(4,128)(2,1)S(1)}, bf16[4,32]{1,0:T(4,128)(2,1)}, u32[]{:S(2)}) copy-start(bf16[4,32]{1,0:T(4,128)(2,1)} %param.4) | copy-start | bytes 772
  256.2 10.0 %collective-permute-start.14 = (bf16[4,28000]{1,0:T(4,128)(2,1)S(1)}, bf16[4,28000]{1,0:T(4,128)(2,1)S(1)}, u32[]{:S(2)}, u32[]{:S(2)}) collective-permute-start(bf16[4,28000]{1,0:T(4,128)(2,1)S(1)} %pad_maximum_fusion.3), channel_id=1, source_target_pairs={{0,8},{1,9},{2,10},{3,11},{4,12},{5,13},{6,14},{7,15},{8,16},{9,17... | collective-permute-start | bytes 672008 | tf_op jit(solution)/shard_map/ppermute | solution.py:12
  258.2 12.7 %copy-start.5 = (bf16[4,800]{1,0:T(4,128)(2,1)}, bf16[4,800]{1,0:T(4,128)(2,1)S(1)}, u32[]{:S(2)}) copy-start(bf16[4,800]{1,0:T(4,128)(2,1)S(1)} %fusion.7) | copy-start | bytes 19204
  266.5 12.5 %collective-permute-start.15 = (bf16[4,28800]{1,0:T(4,128)(2,1)S(1)}, bf16[4,28800]{1,0:T(4,128)(2,1)}, u32[]{:S(2)}, u32[]{:S(2)}) collective-permute-start(bf16[4,28800]{1,0:T(4,128)(2,1)S(1)} %pad_maximum_fusion.2), channel_id=1, source_target_pairs={{0,4},{1,5},{2,6},{3,7},{4,8},{5,9},{6,10},{7,11},{8,12},{9,13},{1... | collective-permute-start | bytes 691208 | tf_op jit(solution)/shard_map/ppermute | solution.py:12
  280.0 12.2 %collective-permute-start.16 = (bf16[4,29200]{1,0:T(4,128)(2,1)S(1)}, bf16[4,29200]{1,0:T(4,128)(2,1)S(1)}, u32[]{:S(2)}, u32[]{:S(2)}) collective-permute-start(bf16[4,29200]{1,0:T(4,128)(2,1)S(1)} %pad_maximum_fusion.1), channel_id=1, source_target_pairs={{0,2},{1,3},{2,4},{3,5},{4,6},{5,7},{6,8},{7,9},{8,10},{9,11},{10,... | collective-permute-start | bytes 700808 | tf_op jit(solution)/shard_map/ppermute | solution.py:12
  292.5 11.6 %collective-permute-start.17 = (bf16[4,29400]{1,0:T(4,128)(2,1)S(1)}, bf16[4,29400]{1,0:T(4,128)(2,1)S(1)}, u32[]{:S(2)}, u32[]{:S(2)}) collective-permute-start(bf16[4,29400]{1,0:T(4,128)(2,1)S(1)} %pad_maximum_fusion), channel_id=1, source_target_pairs={{0,1},{1,2},{2,3},{3,4},{4,5},{5,6},{6,7},{7,8},{8,9},{9,10},{10,1... | collective-permute-start | bytes 705608 | tf_op jit(solution)/shard_map/ppermute | solution.py:12
where the time goes:
time: 306 us; the launch traced here: 305 us
  waiting for transfers between devices  187 us (61%)
  starting transfers between devices  97.8 us (32%)
  other arithmetic  14.1 us (5%)
  local copies, waits for them, and re-layouts  3.27 us (1%)
    ppermute x18, waiting for transfers between devices, from_behind(): lax.ppermute(value, axis, [(source, source + steps) for source in range(f...  187 us
    ppermute x18, starting transfers between devices, from_behind(): lax.ppermute(value, axis, [(source, source + steps) for source in range(f...  97.8 us
    lt x9, other arithmetic, mask_round(): columns < limit  6.22 us
  transfers between devices with their start and end apart: 18, of which 18 were waited for; matrix products, arithmetic and copies ran while one was open for 3% of the time, Pallas kernels for 0%

commit v1 on v0

v1 whole, which is shorter than its diff:
```python
import functools

import jax
import jax.numpy as jnp
from jax import lax
from jax.experimental import pallas as pl
from jax.experimental.pallas import tpu as pltpu
from jax.sharding import PartitionSpec as P

MESH = pl.DeviceIdType.MESH
F32, BF16 = jnp.float32, jnp.bfloat16

CORE, X0, X1, Z0, Z1, Z2, Z3, Y0, Y1 = (1 << b for b in range(9))

ZONES = ((0, 100), (100, 50), (150, 64), (214, 16))
WIDE = (13, 7, 8, 2)
AT = (0, 13, 20, 28)
BLOCKS = 30
COLS = 29400
ENDS = (12800, 19200, 22400, 25600, 27200, 28000, 28800, 29200, 29400)
STARTS = (0,) + ENDS[:-1]
LOC = 4096


def window(zone, i):
    first, tiles = ZONES[zone]
    return first + (tiles * i) // 8


def column_of(zone, core, j):
    shape = (16, 128)
    i = 4 * core + lax.broadcasted_iota(jnp.int32, shape, 0) // 4
    lane = lax.broadcasted_iota(jnp.int32, shape, 1)
    first, tiles = ZONES[zone]
    start = first + (tiles * i) // 8
    end = first + (tiles * (i + 1)) // 8
    return (start + j) * 128 + lane, end * 128


def hops(mask):
    x, y = (mask // X0) % 4, (mask // Y0) % 4
    return (x > 0) + (x == 2) + (y > 0) + (y == 2) + (mask // Z0) % 2


def masks_of(bits):
    found = [0]
    for bit in bits:
        found += [m | bit for m in found]
    return sorted(found[1:], key=hops, reverse=True)


PLANE = masks_of((X0, X1, Z0, Y0, Y1))
PAIR = masks_of((X0, X1, Z0, Y0))
LINE = masks_of((X0, X1, Z0))
DEPTH = [m * Z1 for m in (4, 5, 3, 6, 2, 7, 1)]


def kernel(rhs_hbm, sizes_hbm, xsep_ref, xloc_ref, out_ref,
           rhs_ref, sizes_ref, xs, tail, xl, mine, send_core, recv_core, recv_ab, recv_c, recv_d, part_ab, part_c, deep_ab, deep_c, full,
           small_sem, load_sem, loc_sem, core_send, core_recv, rs_send, rs_recv, z_send, z_recv, ag_send, ag_recv,
           relay_send, relay_recv):
    me = lax.axis_index("leaf")

    def bit(b):
        return (me // b) % 2

    core = bit(CORE)
    y0, y1 = bit(Y0), bit(Y1)
    k = 2 * ((me // X0) % 4) + bit(Z0)
    delta = {b: (1 - 2 * bit(b)) * b for b in (CORE, X0, X1, Z0, Z1, Z2, Z3, Y0, Y1)}

    def partner(mask):
        other = me
        for b, d in delta.items():
            if mask & b:
                other = other + d
        return other

    def remote(src, dst, send, recv, device):
        return pltpu.make_async_remote_copy(
            src_ref=src, dst_ref=dst, send_sem=send, recv_sem=recv, device_id=(device,), device_id_type=MESH
        )

    def drain(ref, sem):
        pltpu.make_async_copy(ref, ref, sem).wait()

    rhs_copy = pltpu.make_async_copy(rhs_hbm, rhs_ref, small_sem.at[0])
    sizes_copy = pltpu.make_async_copy(sizes_hbm, sizes_ref, small_sem.at[1])
    rhs_copy.start()
    sizes_copy.start()

    loads = {}
    for zone in range(4):
        for half in (1, 0):
            owner = core if half == 0 else 1 - core
            group = []
            for s in range(4):
                begin0, begin1 = window(zone, s), window(zone, 4 + s)
                width = WIDE[zone] * 128
                at = AT[zone] * 128
                rows = pl.ds(32 * s, 32)
                sem = load_sem.at[half, zone, s]
                if zone == 3 and s == 3:
                    group.append((begin0, begin1, sem, rows, at, owner))
                    continue
                start = pl.multiple_of((begin0 + owner * (begin1 - begin0)) * 128, 128)
                copy = pltpu.make_async_copy(
                    xsep_ref.at[:, pl.ds(start, width)], xs.at[half, rows, pl.ds(at, width)], sem
                )
                copy.start()
                group.append(copy)
            loads[zone, half] = group

    def last_copies(half, last):
        begin0, begin1, sem, rows, at, owner = loads[3, half][3]
        if not last:
            return [pltpu.make_async_copy(
                xsep_ref.at[:, pl.ds(begin0 * 128, 256)], xs.at[half, rows, pl.ds(at, 256)], sem)]
        rest = COLS - (begin1 + 1) * 128
        return [
            pltpu.make_async_copy(
                xsep_ref.at[:, pl.ds(begin1 * 128, 128)], xs.at[half, rows, pl.ds(at, 128)], sem),
            pltpu.make_async_copy(
                xsep_ref.at[:, pl.ds((begin1 + 1) * 128, rest)], tail, load_sem.at[half, 3, 4]),
        ]

    def last_do(action):
        for half in (0, 1):
            owner = core if half == 0 else 1 - core
            for last in (False, True):
                @pl.when(owner == int(last))
                def _():
                    for copy in last_copies(half, last):
                        action(copy)

    last_do(lambda copy: copy.start())
    loc_copies = [
        pltpu.make_async_copy(xloc_ref.at[:, pl.ds(1024 * s, 1024)], xl.at[pl.ds(32 * s, 32), :], loc_sem.at[s])
        for s in range(4)
    ]
    for copy in loc_copies:
        copy.start()

    barrier = pltpu.get_barrier_semaphore()
    greeted = DEPTH + PLANE + [CORE]
    for mask in greeted:
        pl.semaphore_signal(barrier, inc=1, device_id=(partner(mask),), device_id_type=MESH)

    row = lax.broadcasted_iota(jnp.int32, (16, 128), 0)
    lane = lax.broadcasted_iota(jnp.int32, (16, 128), 1)
    diagonal = row // 4 == lane // 32
    pick_rows = (lax.broadcasted_iota(jnp.int32, (16, 4), 0) % 4 == lax.broadcasted_iota(jnp.int32, (16, 4), 1))
    pick_lanes = (lax.broadcasted_iota(jnp.int32, (32, 128), 1) % 32 == lax.broadcasted_iota(jnp.int32, (32, 128), 0))
    rhs_copy.wait()
    sizes_copy.wait()
    tall = jnp.dot(pick_rows.astype(BF16), rhs_ref[...], preferred_element_type=F32).astype(BF16)
    wide = jnp.dot(tall, pick_lanes.astype(BF16), preferred_element_type=F32)
    rhs16 = jnp.where(diagonal, wide, 0.0).astype(BF16)

    def contributions(zone, half, store):
        columns = pl.ds(AT[zone] * 128, WIDE[zone] * 128)
        product = jnp.dot(rhs16, xs[half, :, columns], preferred_element_type=F32)
        for j in range(WIDE[zone]):
            store[AT[zone] + j] = product[:, 128 * j : 128 * j + 128]

    def place_tail(half):
        @pl.when((core if half == 0 else 1 - core) == 1)
        def _():
            rest = jnp.concatenate([tail[...], jnp.zeros((32, 128 - tail.shape[1]), BF16)], axis=1)
            xs[half, 96:128, BLOCKS * 128 - 128 : BLOCKS * 128] = rest

    for zone in range(4):
        for half in (1, 0):
            for copy in loads[zone, half]:
                if not isinstance(copy, tuple):
                    copy.wait()
        if zone == 3:
            last_do(lambda copy: copy.wait())
            place_tail(1)
            place_tail(0)
        contributions(zone, 1, send_core)
        contributions(zone, 0, mine)

    pl.semaphore_wait(barrier, len(greeted))

    sibling = partner(CORE)
    core_copies = []
    for zone in range(4):
        blocks = pl.ds(AT[zone], WIDE[zone])
        copy = remote(send_core.at[blocks], recv_core.at[blocks], core_send.at[zone], core_recv.at[zone], sibling)
        copy.start()
        core_copies.append(copy)

    base = me - me % Z1 + core - y1 * Y1 - y0 * Y0

    def place(kk):
        return (kk // 2) * X0 + (kk % 2) * Z0

    def owner_a(a):
        return base + (a % 2) * Y1 + core * Y0 + place(a // 2)

    def owner_b(b):
        return base + y1 * Y1 + (1 - core) * Y0 + place(b)

    def owner_c(d):
        return base + y1 * Y1 + y0 * Y0 + place(d)

    role_a = y0 == core
    a_mine = 2 * k + y1
    owns_a = jnp.logical_and(role_a, a_mine < WIDE[0])
    owns_b = jnp.logical_and(jnp.logical_not(role_a), k < WIDE[1])
    slot_a = 16 * y1 + 8 * y0 + k
    slot_b = 8 * y0 + k

    def scatter(zone, count, owner, slot, landing, sem):
        for j in range(count):
            block = AT[zone] + j
            to = owner(j)

            @pl.when(to == me)
            def _():
                landing[slot] = mine[block]

            @pl.when(to != me)
            def _():
                remote(mine.at[block], landing.at[slot], rs_send.at[sem], rs_recv.at[sem], to).start()

    for zone in range(4):
        core_copies[zone].wait_recv()
        for j in range(WIDE[zone]):
            block = AT[zone] + j
            mine[block] = mine[block] + recv_core[block]
        if zone == 0:
            scatter(0, WIDE[0], owner_a, slot_a, recv_ab, 0)
        elif zone == 1:
            scatter(1, WIDE[1], owner_b, slot_b, recv_ab, 1)
        elif zone == 2:
            scatter(2, WIDE[2], owner_c, k, recv_c, 2)

    def d_copy(n, mask):
        return remote(mine.at[pl.ds(AT[3], 2)], recv_d.at[n], rs_send.at[3 + n], rs_recv.at[3 + n], partner(mask))

    def d_do(action):
        for n, mask in enumerate(LINE):
            if mask & Z0:
                @pl.when(core == 0)
                def _():
                    action(d_copy(n, mask))
            else:
                action(d_copy(n, mask))

    d_do(lambda copy: copy.start())

    def total(landing, count):
        acc = [landing[i] for i in range(4)]
        for i in range(4, count):
            acc[i % 4] = acc[i % 4] + landing[i]
        return (acc[0] + acc[1]) + (acc[2] + acc[3])

    def deep_copies(src, landing, at):
        return [
            remote(src, landing.at[m // Z1 - 1], z_send.at[at], z_recv.at[at], partner(m)) for m in DEPTH
        ]

    @pl.when(owns_a)
    def _():
        drain(recv_ab.at[pl.ds(0, 31)], rs_recv.at[0])
        part_ab[...] = total(recv_ab, 32)

    @pl.when(owns_b)
    def _():
        drain(recv_ab.at[pl.ds(0, 15)], rs_recv.at[1])
        part_ab[...] = total(recv_ab, 16)

    owns_ab = jnp.logical_or(owns_a, owns_b)

    @pl.when(owns_ab)
    def _():
        for copy in deep_copies(part_ab, deep_ab, 0):
            copy.start()

    drain(recv_c.at[pl.ds(0, 7)], rs_recv.at[2])
    part_c[...] = total(recv_c, 8)
    deep_c_copies = deep_copies(part_c, deep_c, 1)
    for m, copy in zip(DEPTH, deep_c_copies):
        if m & Z3:
            @pl.when(core == 0)
            def _():
                copy.start()
        else:
            copy.start()

    def active(columns, zone):
        lo, hi = ZONES[zone][0] * 128, sum(ZONES[zone]) * 128
        keep = None
        for level in range(9):
            if STARTS[level] < hi and ENDS[level] > lo:
                limit = STARTS[level] + sizes_ref[level]
                inside = jnp.logical_and(
                    jnp.logical_and(columns >= STARTS[level], columns < ENDS[level]), columns < limit)
                keep = inside if keep is None else jnp.logical_or(keep, inside)
        return keep

    def rounded(values, columns, end, zone):
        keep = jnp.logical_and(active(columns, zone), columns < end)
        return jnp.where(keep, values, 0.0).astype(BF16)

    d_do(lambda copy: copy.wait_recv())
    for j in range(2):
        columns, end = column_of(3, core, j)
        value = mine[AT[3] + j]
        for n, mask in enumerate(LINE):
            if mask & Z0:
                bound = jnp.where(core == 0, ENDS[5], 0)
            else:
                bound = ENDS[6] if mask & X1 else ENDS[7]
            value = value + jnp.where(columns < bound, recv_d[n, j], 0.0)
        full[0, AT[3] + j] = rounded(value, columns, end, 3)

    def relay(zone, at):
        blocks = pl.ds(AT[zone], WIDE[zone])
        return remote(full.at[0, blocks], full.at[1, blocks], relay_send.at[at], relay_recv.at[at], sibling)

    relay(3, 3).start()

    for copy in loc_copies:
        copy.wait()
    interior = jnp.dot(rhs16, xl[...], preferred_element_type=F32).astype(BF16)
    contract = (((1,), (1,)), ((), ()))
    acc = lax.dot_general(interior, xl[...], contract, preferred_element_type=F32)

    def product(zone, half):
        blocks = jnp.concatenate([full[half, AT[zone] + j] for j in range(WIDE[zone])], axis=1)
        columns = pl.ds(AT[zone] * 128, WIDE[zone] * 128)
        return lax.dot_general(blocks, xs[half, :, columns], contract, preferred_element_type=F32)

    def deep_total(part, landing):
        value = part[...]
        for i in range(7):
            value = value + landing[i]
        return value

    def gather(block, masks, sem):
        for mask in masks:
            remote(full.at[0, block], full.at[0, block], ag_send.at[sem], ag_recv.at[sem], partner(mask)).start()

    @pl.when(owns_ab)
    def _():
        drain(deep_ab, z_recv.at[0])

    @pl.when(owns_a)
    def _():
        columns, end = column_of(0, core, a_mine)
        full[0, a_mine] = rounded(deep_total(part_ab, deep_ab), columns, end, 0)
        gather(a_mine, PLANE, 0)

    @pl.when(owns_b)
    def _():
        columns, end = column_of(1, core, k)
        full[0, AT[1] + k] = rounded(deep_total(part_ab, deep_ab), columns, end, 1)
        gather(AT[1] + k, PAIR, 1)

    @pl.when(core == 0)
    def _():
        drain(deep_c, z_recv.at[1])

    @pl.when(core == 1)
    def _():
        drain(deep_c.at[pl.ds(0, 3)], z_recv.at[1])

    columns, end = column_of(2, core, k)
    value = part_c[...]
    for m in range(1, 8):
        bound = ENDS[4] if m == 1 else ENDS[3] if m < 4 else jnp.where(core == 0, ENDS[2], 0)
        value = value + jnp.where(columns < bound, deep_c[m - 1], 0.0)
    full[0, AT[2] + k] = rounded(value, columns, end, 2)
    gather(AT[2] + k, LINE, 2)

    drain(full.at[0, pl.ds(AT[2], 7)], ag_recv.at[2])
    relay(2, 2).start()
    acc = acc + product(2, 0) + product(3, 0)
    relay(3, 3).wait_recv()
    acc = acc + product(3, 1)
    relay(2, 2).wait_recv()
    acc = acc + product(2, 1)

    def drain_gather(owns, zone):
        @pl.when(owns)
        def _():
            drain(full.at[0, pl.ds(AT[zone], WIDE[zone] - 1)], ag_recv.at[zone])

        @pl.when(jnp.logical_not(owns))
        def _():
            drain(full.at[0, pl.ds(AT[zone], WIDE[zone])], ag_recv.at[zone])

    drain_gather(owns_b, 1)
    relay(1, 1).start()
    acc = acc + product(1, 0)
    drain_gather(owns_a, 0)
    relay(0, 0).start()
    acc = acc + product(0, 0)
    relay(1, 1).wait_recv()
    acc = acc + product(1, 1)
    relay(0, 0).wait_recv()
    acc = acc + product(0, 1)
    out_ref[...] = (acc[0:4, 0:32] + acc[4:8, 32:64]) + (acc[8:12, 64:96] + acc[12:16, 96:128])

    for zone in range(4):
        core_copies[zone].wait_send()
        relay(zone, zone).wait_send()

    def drain_scatter(owns, zone):
        @pl.when(owns)
        def _():
            drain(mine.at[pl.ds(0, WIDE[zone] - 1)], rs_send.at[zone])

        @pl.when(jnp.logical_not(owns))
        def _():
            drain(mine.at[pl.ds(0, WIDE[zone])], rs_send.at[zone])

    drain_scatter(owns_a, 0)
    drain_scatter(owns_b, 1)
    drain(mine.at[pl.ds(0, 7)], rs_send.at[2])
    d_do(lambda copy: copy.wait_send())

    @pl.when(owns_ab)
    def _():
        drain(deep_ab, z_send.at[0])

    @pl.when(core == 0)
    def _():
        drain(deep_c, z_send.at[1])

    @pl.when(core == 1)
    def _():
        drain(deep_c.at[pl.ds(0, 3)], z_send.at[1])

    @pl.when(owns_a)
    def _():
        for _ in range(1):
            drain(full.at[0, pl.ds(0, 30)], ag_send.at[0])
            drain(full.at[0, pl.ds(0, 1)], ag_send.at[0])

    @pl.when(owns_b)
    def _():
        drain(full.at[0, pl.ds(0, 15)], ag_send.at[1])

    drain(full.at[0, pl.ds(0, 7)], ag_send.at[2])


def body(rhs, x_sep, x_loc, sep_sizes):
    vmem, hbm = pl.BlockSpec(memory_space=pltpu.VMEM), pl.BlockSpec(memory_space=pltpu.HBM)
    dma = pltpu.SemaphoreType.DMA
    blocks = functools.partial(pltpu.VMEM, dtype=F32)
    return pl.pallas_call(
        kernel,
        out_shape=jax.ShapeDtypeStruct((4, 32), F32),
        in_specs=[hbm] * 4,
        out_specs=vmem,
        scratch_shapes=[
            pltpu.VMEM((4, 32), BF16),
            pltpu.SMEM((9,), jnp.int32),
            pltpu.VMEM((2, 128, BLOCKS * 128), BF16),
            pltpu.VMEM((32, COLS % 128), BF16),
            pltpu.VMEM((128, LOC // 4), BF16),
            blocks((BLOCKS, 16, 128)),
            blocks((BLOCKS, 16, 128)),
            blocks((BLOCKS, 16, 128)),
            blocks((32, 16, 128)),
            blocks((8, 16, 128)),
            blocks((7, 2, 16, 128)),
            blocks((16, 128)),
            blocks((16, 128)),
            blocks((7, 16, 128)),
            blocks((7, 16, 128)),
            pltpu.VMEM((2, BLOCKS, 16, 128), BF16),
            dma((2,)),
            dma((2, 4, 5)),
            dma((4,)),
            dma((4,)),
            dma((4,)),
            dma((10,)),
            dma((10,)),
            dma((2,)),
            dma((2,)),
            dma((3,)),
            dma((3,)),
            dma((4,)),
            dma((4,)),
        ],
        compiler_params=pltpu.CompilerParams(
            collective_id=0, has_side_effects=True, vmem_limit_bytes=60 * 1024 * 1024
        ),
        name="xxt",
    )(rhs, sep_sizes, x_sep, x_loc)


def solution(mesh):
    placed = (P(None, "leaf"), P("leaf", None), P("leaf", None), P())
    return jax.shard_map(
        body, mesh=mesh, in_specs=placed, out_specs=P(None, "leaf"), check_vma=False
    )
```

time: 306 us -> 41.4 us (0.14)
  the two profiles are of different devices: /device:TPU:16 before, /device:TPU:1 now
where the time goes in v1:
time: 41.4 us; the launch traced here: 41.2 us
  Pallas kernels  39.9 us (96%)
  local copies, waits for them, and re-layouts  1.26 us (3%)
    pallas_call x1, Pallas kernels, body(): pl.pallas_call(kernel, out_shape=jax.ShapeDtypeStruct((4, 32), F32), in_s...  39.9 us
    unnamed x1, local copies, waits for them, and re-layouts  1.26 us

profile of v1, /device:TPU:1, one launch (start us, length us, event | category | flops | bytes accessed | tf_op | source)
XLA Modules:
  0.0 41.2 jit_solution(4106080573774281439)
XLA Ops:
  0.0 39.9 %xxt.1 = f32[4,32]{1,0:T(4,128)} custom-call(bf16[4,32]{1,0:T(4,128)(2,1)} %rhs_hbm.1, s32[9]{0:T(128)} %sizes_hbm.1, bf16[32,29400]{1,0:T(8,128)(2,1)} %xsep_ref.1, bf16[32,4096]{1,0:T(8,128)(2,1)} %xloc_ref.1), custom_call_target="tpu_custom_call" | custom-call | tf_op jit(solution)/shard_map/xxt/pallas_call | solution.py:455
  39.9 1.3 %copy.6 = f32[4,32]{1,0:T(4,128)} copy(f32[4,32]{1,0:T(4,128)} %xxt.1) | data formatting | bytes 1024

commit v2 on v1

--- a/solution.py
+++ b/solution.py
@@ -58,7 +58,7 @@
 def kernel(rhs_hbm, sizes_hbm, xsep_ref, xloc_ref, out_ref,
            rhs_ref, sizes_ref, xs, tail, xl, mine, send_core, recv_core, recv_ab, recv_c, recv_d, part_ab, part_c, deep_ab, deep_c, full,
            small_sem, load_sem, loc_sem, core_send, core_recv, rs_send, rs_recv, z_send, z_recv, ag_send, ag_recv,
-           relay_send, relay_recv):
+           relay_send, relay_recv, token):
     me = lax.axis_index("leaf")
 
     def bit(b):
@@ -83,6 +83,16 @@
 
     def drain(ref, sem):
         pltpu.make_async_copy(ref, ref, sem).wait()
+
+    depth = (me // Z1) % 8
+
+    def along(step):
+        return me + ((depth + step + 8) % 8 - depth) * Z1
+
+    barrier = pltpu.get_barrier_semaphore()
+    greeted = [partner(m) for m in PLANE] + [along(s) for s in (2, -2, 1, -1)] + [partner(CORE)]
+    for device in greeted:
+        pl.semaphore_signal(barrier, inc=1, device_id=(device,), device_id_type=MESH)
 
     rhs_copy = pltpu.make_async_copy(rhs_hbm, rhs_ref, small_sem.at[0])
     sizes_copy = pltpu.make_async_copy(sizes_hbm, sizes_ref, small_sem.at[1])
@@ -141,11 +151,6 @@
     for copy in loc_copies:
         copy.start()
 
-    barrier = pltpu.get_barrier_semaphore()
-    greeted = DEPTH + PLANE + [CORE]
-    for mask in greeted:
-        pl.semaphore_signal(barrier, inc=1, device_id=(partner(mask),), device_id_type=MESH)
-
     row = lax.broadcasted_iota(jnp.int32, (16, 128), 0)
     lane = lax.broadcasted_iota(jnp.int32, (16, 128), 1)
     diagonal = row // 4 == lane // 32
@@ -182,6 +187,8 @@
         contributions(zone, 0, mine)
 
     pl.semaphore_wait(barrier, len(greeted))
+    for step in (2, -2):
+        pl.semaphore_signal(token, inc=1, device_id=(along(step),), device_id_type=MESH)
 
     sibling = partner(CORE)
     core_copies = []
@@ -262,22 +269,7 @@
             remote(src, landing.at[m // Z1 - 1], z_send.at[at], z_recv.at[at], partner(m)) for m in DEPTH
         ]
 
-    @pl.when(owns_a)
-    def _():
-        drain(recv_ab.at[pl.ds(0, 31)], rs_recv.at[0])
-        part_ab[...] = total(recv_ab, 32)
-
-    @pl.when(owns_b)
-    def _():
-        drain(recv_ab.at[pl.ds(0, 15)], rs_recv.at[1])
-        part_ab[...] = total(recv_ab, 16)
-
-    owns_ab = jnp.logical_or(owns_a, owns_b)
-
-    @pl.when(owns_ab)
-    def _():
-        for copy in deep_copies(part_ab, deep_ab, 0):
-            copy.start()
+    pl.semaphore_wait(token, 2)
 
     drain(recv_c.at[pl.ds(0, 7)], rs_recv.at[2])
     part_c[...] = total(recv_c, 8)
@@ -288,6 +280,23 @@
             def _():
                 copy.start()
         else:
+            copy.start()
+
+    @pl.when(owns_a)
+    def _():
+        drain(recv_ab.at[pl.ds(0, 31)], rs_recv.at[0])
+        part_ab[...] = total(recv_ab, 32)
+
+    @pl.when(owns_b)
+    def _():
+        drain(recv_ab.at[pl.ds(0, 15)], rs_recv.at[1])
+        part_ab[...] = total(recv_ab, 16)
+
+    owns_ab = jnp.logical_or(owns_a, owns_b)
+
+    @pl.when(owns_ab)
+    def _():
+        for copy in deep_copies(part_ab, deep_ab, 0):
             copy.start()
 
     def active(columns, zone):
@@ -344,22 +353,6 @@
         for mask in masks:
             remote(full.at[0, block], full.at[0, block], ag_send.at[sem], ag_recv.at[sem], partner(mask)).start()
 
-    @pl.when(owns_ab)
-    def _():
-        drain(deep_ab, z_recv.at[0])
-
-    @pl.when(owns_a)
-    def _():
-        columns, end = column_of(0, core, a_mine)
-        full[0, a_mine] = rounded(deep_total(part_ab, deep_ab), columns, end, 0)
-        gather(a_mine, PLANE, 0)
-
-    @pl.when(owns_b)
-    def _():
-        columns, end = column_of(1, core, k)
-        full[0, AT[1] + k] = rounded(deep_total(part_ab, deep_ab), columns, end, 1)
-        gather(AT[1] + k, PAIR, 1)
-
     @pl.when(core == 0)
     def _():
         drain(deep_c, z_recv.at[1])
@@ -375,6 +368,22 @@
         value = value + jnp.where(columns < bound, deep_c[m - 1], 0.0)
     full[0, AT[2] + k] = rounded(value, columns, end, 2)
     gather(AT[2] + k, LINE, 2)
+
+    @pl.when(owns_ab)
+    def _():
+        drain(deep_ab, z_recv.at[0])
+
+    @pl.when(owns_a)
+    def _():
+        columns, end = column_of(0, core, a_mine)
+        full[0, a_mine] = rounded(deep_total(part_ab, deep_ab), columns, end, 0)
+        gather(a_mine, PLANE, 0)
+
+    @pl.when(owns_b)
+    def _():
+        columns, end = column_of(1, core, k)
+        full[0, AT[1] + k] = rounded(deep_total(part_ab, deep_ab), columns, end, 1)
+        gather(AT[1] + k, PAIR, 1)
 
     drain(full.at[0, pl.ds(AT[2], 7)], ag_recv.at[2])
     relay(2, 2).start()
@@ -454,7 +463,7 @@
     blocks = functools.partial(pltpu.VMEM, dtype=F32)
     return pl.pallas_call(
         kernel,
-        out_shape=jax.ShapeDtypeStruct((4, 32), F32),
+        out_shape=pltpu.VMEM((4, 32), F32),
         in_specs=[hbm] * 4,
         out_specs=vmem,
         scratch_shapes=[
@@ -487,6 +496,7 @@
             dma((3,)),
             dma((4,)),
             dma((4,)),
+            pltpu.SemaphoreType.REGULAR,
         ],
         compiler_params=pltpu.CompilerParams(
             collective_id=0, has_side_effects=True, vmem_limit_bytes=60 * 1024 * 1024

time: 41.4 us -> 40.4 us (0.976)
  local copies, waits for them, and re-layouts: 1.26 us -> 0.58 us
    unnamed x1, local copies, waits for them, and re-layouts: 1.26 us -> 0.58 us
where the time goes in v2:
time: 40.4 us; the launch traced here: 40.3 us
  Pallas kernels  39.7 us (98%)
  local copies, waits for them, and re-layouts  0.58 us (1%)
    pallas_call x1, Pallas kernels, body(): pl.pallas_call(kernel, out_shape=pltpu.VMEM((4, 32), F32), in_specs=[hbm]...  39.7 us

profile of v2, /device:TPU:1, one launch (start us, length us, event | category | flops | bytes accessed | tf_op | source)
XLA Modules:
  0.0 40.3 jit_solution(4631113913318326297)
XLA Ops:
  0.0 39.7 %xxt.1 = f32[4,32]{1,0:T(4,128)S(1)} custom-call(bf16[4,32]{1,0:T(4,128)(2,1)} %rhs_hbm.1, s32[9]{0:T(128)} %sizes_hbm.1, bf16[32,29400]{1,0:T(8,128)(2,1)} %xsep_ref.1, bf16[32,4096]{1,0:T(8,128)(2,1)} %xloc_ref.1), custom_call_target="tpu_custom_call" | custom-call | tf_op jit(solution)/shard_map/xxt/pallas_call | solution.py:464
  39.7 0.6 %copy.6 = f32[4,32]{1,0:T(4,128)} copy(f32[4,32]{1,0:T(4,128)S(1)} %xxt.1) | data formatting | bytes 1024

commit v3 on v2

--- a/solution.py
+++ b/solution.py
@@ -12,10 +12,11 @@
 
 CORE, X0, X1, Z0, Z1, Z2, Z3, Y0, Y1 = (1 << b for b in range(9))
 
-ZONES = ((0, 100), (100, 50), (150, 64), (214, 16))
-WIDE = (13, 7, 8, 2)
+ZONES = ((0, 100), (100, 50), (150, 64), (212, 18))
+WIDE = (13, 7, 8, 3)
 AT = (0, 13, 20, 28)
-BLOCKS = 30
+BLOCKS = 31
+KEEP = ((0, 12800), (12800, 19200), (19200, 27200), (27200, 29400))
 COLS = 29400
 ENDS = (12800, 19200, 22400, 25600, 27200, 28000, 28800, 29200, 29400)
 STARTS = (0,) + ENDS[:-1]
@@ -38,8 +39,8 @@
 
 
 def hops(mask):
-    x, y = (mask // X0) % 4, (mask // Y0) % 4
-    return (x > 0) + (x == 2) + (y > 0) + (y == 2) + (mask // Z0) % 2
+    x, y, z = (mask // X0) % 4, (mask // Y0) % 4, (mask // Z0) % 4
+    return (x > 0) + (x == 2) + (y > 0) + (y == 2) + z
 
 
 def masks_of(bits):
@@ -52,7 +53,9 @@
 PLANE = masks_of((X0, X1, Z0, Y0, Y1))
 PAIR = masks_of((X0, X1, Z0, Y0))
 LINE = masks_of((X0, X1, Z0))
+SLAB = masks_of((X0, X1, Z0, Z1))
 DEPTH = [m * Z1 for m in (4, 5, 3, 6, 2, 7, 1)]
+DEPTH_C = [m * Z1 for m in (4, 2, 6)]
 
 
 def kernel(rhs_hbm, sizes_hbm, xsep_ref, xloc_ref, out_ref,
@@ -65,7 +68,7 @@
         return (me // b) % 2
 
     core = bit(CORE)
-    y0, y1 = bit(Y0), bit(Y1)
+    y0, y1, z1 = bit(Y0), bit(Y1), bit(Z1)
     k = 2 * ((me // X0) % 4) + bit(Z0)
     delta = {b: (1 - 2 * bit(b)) * b for b in (CORE, X0, X1, Z0, Z1, Z2, Z3, Y0, Y1)}
 
@@ -90,7 +93,8 @@
         return me + ((depth + step + 8) % 8 - depth) * Z1
 
     barrier = pltpu.get_barrier_semaphore()
-    greeted = [partner(m) for m in PLANE] + [along(s) for s in (2, -2, 1, -1)] + [partner(CORE)]
+    greeted = [partner(m) for m in PLANE + [m | Z1 for m in LINE]]
+    greeted += [along(s) for s in (2, -2, 1, -1)] + [partner(CORE)]
     for device in greeted:
         pl.semaphore_signal(barrier, inc=1, device_id=(device,), device_id_type=MESH)
 
@@ -125,13 +129,13 @@
         begin0, begin1, sem, rows, at, owner = loads[3, half][3]
         if not last:
             return [pltpu.make_async_copy(
-                xsep_ref.at[:, pl.ds(begin0 * 128, 256)], xs.at[half, rows, pl.ds(at, 256)], sem)]
-        rest = COLS - (begin1 + 1) * 128
+                xsep_ref.at[:, pl.ds(begin0 * 128, 384)], xs.at[half, rows, pl.ds(at, 384)], sem)]
+        rest = COLS - (begin1 + 2) * 128
         return [
             pltpu.make_async_copy(
-                xsep_ref.at[:, pl.ds(begin1 * 128, 128)], xs.at[half, rows, pl.ds(at, 128)], sem),
+                xsep_ref.at[:, pl.ds(begin1 * 128, 256)], xs.at[half, rows, pl.ds(at, 256)], sem),
             pltpu.make_async_copy(
-                xsep_ref.at[:, pl.ds((begin1 + 1) * 128, rest)], tail, load_sem.at[half, 3, 4]),
+                xsep_ref.at[:, pl.ds((begin1 + 2) * 128, rest)], tail, load_sem.at[half, 3, 4]),
         ]
 
     def last_do(action):
@@ -210,7 +214,7 @@
         return base + y1 * Y1 + (1 - core) * Y0 + place(b)
 
     def owner_c(d):
-        return base + y1 * Y1 + y0 * Y0 + place(d)
+        return base + y1 * Y1 + y0 * Y0 + (core - z1) * Z1 + place(d)
 
     role_a = y0 == core
     a_mine = 2 * k + y1
@@ -218,6 +222,8 @@
     owns_b = jnp.logical_and(jnp.logical_not(role_a), k < WIDE[1])
     slot_a = 16 * y1 + 8 * y0 + k
     slot_b = 8 * y0 + k
+    slot_c = 8 * z1 + k
+    owns_c = z1 == core
 
     def scatter(zone, count, owner, slot, landing, sem):
         for j in range(count):
@@ -242,10 +248,10 @@
         elif zone == 1:
             scatter(1, WIDE[1], owner_b, slot_b, recv_ab, 1)
         elif zone == 2:
-            scatter(2, WIDE[2], owner_c, k, recv_c, 2)
+            scatter(2, WIDE[2], owner_c, slot_c, recv_c, 2)
 
     def d_copy(n, mask):
-        return remote(mine.at[pl.ds(AT[3], 2)], recv_d.at[n], rs_send.at[3 + n], rs_recv.at[3 + n], partner(mask))
+        return remote(mine.at[pl.ds(AT[3], WIDE[3])], recv_d.at[n], rs_send.at[3 + n], rs_recv.at[3 + n], partner(mask))
 
     def d_do(action):
         for n, mask in enumerate(LINE):
@@ -256,8 +262,6 @@
             else:
                 action(d_copy(n, mask))
 
-    d_do(lambda copy: copy.start())
-
     def total(landing, count):
         acc = [landing[i] for i in range(4)]
         for i in range(4, count):
@@ -271,17 +275,6 @@
 
     pl.semaphore_wait(token, 2)
 
-    drain(recv_c.at[pl.ds(0, 7)], rs_recv.at[2])
-    part_c[...] = total(recv_c, 8)
-    deep_c_copies = deep_copies(part_c, deep_c, 1)
-    for m, copy in zip(DEPTH, deep_c_copies):
-        if m & Z3:
-            @pl.when(core == 0)
-            def _():
-                copy.start()
-        else:
-            copy.start()
-
     @pl.when(owns_a)
     def _():
         drain(recv_ab.at[pl.ds(0, 31)], rs_recv.at[0])
@@ -298,6 +291,24 @@
     def _():
         for copy in deep_copies(part_ab, deep_ab, 0):
             copy.start()
+
+    def c_far(action):
+        for m in DEPTH_C:
+            if m & Z3:
+                @pl.when(core == 0)
+                def _():
+                    action(m)
+            else:
+                action(m)
+
+    @pl.when(owns_c)
+    def _():
+        drain(recv_c.at[pl.ds(0, 15)], rs_recv.at[2])
+        part_c[...] = total(recv_c, 16)
+        c_far(lambda m: remote(
+            part_c, deep_c.at[m // Z2 - 1], z_send.at[1], z_recv.at[1], partner(m)).start())
+
+    d_do(lambda copy: copy.start())
 
     def active(columns, zone):
         lo, hi = ZONES[zone][0] * 128, sum(ZONES[zone]) * 128
@@ -308,14 +319,15 @@
                 inside = jnp.logical_and(
                     jnp.logical_and(columns >= STARTS[level], columns < ENDS[level]), columns < limit)
                 keep = inside if keep is None else jnp.logical_or(keep, inside)
-        return keep
+        lo, hi = KEEP[zone]
+        return jnp.logical_and(keep, jnp.logical_and(columns >= lo, columns < hi))
 
     def rounded(values, columns, end, zone):
         keep = jnp.logical_and(active(columns, zone), columns < end)
         return jnp.where(keep, values, 0.0).astype(BF16)
 
     d_do(lambda copy: copy.wait_recv())
-    for j in range(2):
+    for j in range(WIDE[3]):
         columns, end = column_of(3, core, j)
         value = mine[AT[3] + j]
         for n, mask in enumerate(LINE):
@@ -351,23 +363,9 @@
 
     def gather(block, masks, sem):
         for mask in masks:
-            remote(full.at[0, block], full.at[0, block], ag_send.at[sem], ag_recv.at[sem], partner(mask)).start()
-
-    @pl.when(core == 0)
-    def _():
-        drain(deep_c, z_recv.at[1])
-
-    @pl.when(core == 1)
-    def _():
-        drain(deep_c.at[pl.ds(0, 3)], z_recv.at[1])
-
-    columns, end = column_of(2, core, k)
-    value = part_c[...]
-    for m in range(1, 8):
-        bound = ENDS[4] if m == 1 else ENDS[3] if m < 4 else jnp.where(core == 0, ENDS[2], 0)
-        value = value + jnp.where(columns < bound, deep_c[m - 1], 0.0)
-    full[0, AT[2] + k] = rounded(value, columns, end, 2)
-    gather(AT[2] + k, LINE, 2)
+            remote(full.at[0, block], full.at[0, block], ag_send.at[sem], ag_recv.at[0, sem], partner(mask)).start()
+            remote(full.at[0, block], full.at[1, block], ag_send.at[sem], ag_recv.at[1, sem], partner(mask | CORE)).start()
+        remote(full.at[0, block], full.at[1, block], ag_send.at[sem], ag_recv.at[1, sem], partner(CORE)).start()
 
     @pl.when(owns_ab)
     def _():
@@ -385,76 +383,93 @@
         full[0, AT[1] + k] = rounded(deep_total(part_ab, deep_ab), columns, end, 1)
         gather(AT[1] + k, PAIR, 1)
 
-    drain(full.at[0, pl.ds(AT[2], 7)], ag_recv.at[2])
-    relay(2, 2).start()
-    acc = acc + product(2, 0) + product(3, 0)
+    @pl.when(owns_c)
+    def _():
+        @pl.when(core == 0)
+        def _():
+            drain(deep_c, z_recv.at[1])
+
+        @pl.when(core == 1)
+        def _():
+            drain(deep_c.at[pl.ds(0, 1)], z_recv.at[1])
+
+        columns, end = column_of(2, core, k)
+        value = part_c[...]
+        for m in range(1, 4):
+            bound = ENDS[3] if m == 1 else jnp.where(core == 0, ENDS[2], 0)
+            value = value + jnp.where(columns < bound, deep_c[m - 1], 0.0)
+        full[0, AT[2] + k] = rounded(value, columns, end, 2)
+        gather(AT[2] + k, SLAB, 2)
+
+    acc = acc + product(3, 0)
     relay(3, 3).wait_recv()
     acc = acc + product(3, 1)
-    relay(2, 2).wait_recv()
-    acc = acc + product(2, 1)
+
+    for zone in range(4):
+        core_copies[zone].wait_send()
+    relay(3, 3).wait_send()
+
+    def drain_scatter(owns, zone):
+        @pl.when(owns)
+        def _():
+            drain(mine.at[pl.ds(0, WIDE[zone] - 1)], rs_send.at[zone])
+
+        @pl.when(jnp.logical_not(owns))
+        def _():
+            drain(mine.at[pl.ds(0, WIDE[zone])], rs_send.at[zone])
+
+    drain_scatter(owns_a, 0)
+    drain_scatter(owns_b, 1)
+    drain_scatter(owns_c, 2)
+    d_do(lambda copy: copy.wait_send())
+
+    @pl.when(owns_ab)
+    def _():
+        drain(deep_ab, z_send.at[0])
+
+    @pl.when(jnp.logical_and(owns_c, core == 0))
+    def _():
+        drain(deep_c, z_send.at[1])
+
+    @pl.when(jnp.logical_and(owns_c, core == 1))
+    def _():
+        drain(deep_c.at[pl.ds(0, 1)], z_send.at[1])
 
     def drain_gather(owns, zone):
         @pl.when(owns)
         def _():
-            drain(full.at[0, pl.ds(AT[zone], WIDE[zone] - 1)], ag_recv.at[zone])
+            drain(full.at[0, pl.ds(AT[zone], WIDE[zone] - 1)], ag_recv.at[0, zone])
 
         @pl.when(jnp.logical_not(owns))
         def _():
-            drain(full.at[0, pl.ds(AT[zone], WIDE[zone])], ag_recv.at[zone])
+            drain(full.at[0, pl.ds(AT[zone], WIDE[zone])], ag_recv.at[0, zone])
 
     drain_gather(owns_b, 1)
-    relay(1, 1).start()
     acc = acc + product(1, 0)
+    drain(full.at[1, pl.ds(AT[1], WIDE[1])], ag_recv.at[1, 1])
+    acc = acc + product(1, 1)
+    drain_gather(owns_c, 2)
+    acc = acc + product(2, 0)
+    drain(full.at[1, pl.ds(AT[2], WIDE[2])], ag_recv.at[1, 2])
+    acc = acc + product(2, 1)
     drain_gather(owns_a, 0)
-    relay(0, 0).start()
     acc = acc + product(0, 0)
-    relay(1, 1).wait_recv()
-    acc = acc + product(1, 1)
-    relay(0, 0).wait_recv()
+    drain(full.at[1, pl.ds(AT[0], WIDE[0])], ag_recv.at[1, 0])
     acc = acc + product(0, 1)
     out_ref[...] = (acc[0:4, 0:32] + acc[4:8, 32:64]) + (acc[8:12, 64:96] + acc[12:16, 96:128])
 
-    for zone in range(4):
-        core_copies[zone].wait_send()
-        relay(zone, zone).wait_send()
-
-    def drain_scatter(owns, zone):
-        @pl.when(owns)
-        def _():
-            drain(mine.at[pl.ds(0, WIDE[zone] - 1)], rs_send.at[zone])
-
-        @pl.when(jnp.logical_not(owns))
-        def _():
-            drain(mine.at[pl.ds(0, WIDE[zone])], rs_send.at[zone])
-
-    drain_scatter(owns_a, 0)
-    drain_scatter(owns_b, 1)
-    drain(mine.at[pl.ds(0, 7)], rs_send.at[2])
-    d_do(lambda copy: copy.wait_send())
-
-    @pl.when(owns_ab)
-    def _():
-        drain(deep_ab, z_send.at[0])
-
-    @pl.when(core == 0)
-    def _():
-        drain(deep_c, z_send.at[1])
-
-    @pl.when(core == 1)
-    def _():
-        drain(deep_c.at[pl.ds(0, 3)], z_send.at[1])
-
     @pl.when(owns_a)
     def _():
-        for _ in range(1):
-            drain(full.at[0, pl.ds(0, 30)], ag_send.at[0])
-            drain(full.at[0, pl.ds(0, 1)], ag_send.at[0])
+        drain(full, ag_send.at[0])
+        drain(full.at[0, pl.ds(0, 1)], ag_send.at[0])
 
     @pl.when(owns_b)
     def _():
-        drain(full.at[0, pl.ds(0, 15)], ag_send.at[1])
-
-    drain(full.at[0, pl.ds(0, 7)], ag_send.at[2])
+        drain(full.at[0, pl.ds(0, 31)], ag_send.at[1])
+
+    @pl.when(owns_c)
+    def _():
+        drain(full.at[0, pl.ds(0, 31)], ag_send.at[2])
 
 
 def body(rhs, x_sep, x_loc, sep_sizes):
@@ -476,12 +491,12 @@
             blocks((BLOCKS, 16, 128)),
             blocks((BLOCKS, 16, 128)),
             blocks((32, 16, 128)),
-            blocks((8, 16, 128)),
-            blocks((7, 2, 16, 128)),
+            blocks((16, 16, 128)),
+            blocks((7, WIDE[3], 16, 128)),
             blocks((16, 128)),
             blocks((16, 128)),
             blocks((7, 16, 128)),
-            blocks((7, 16, 128)),
+            blocks((3, 16, 128)),
             pltpu.VMEM((2, BLOCKS, 16, 128), BF16),
             dma((2,)),
             dma((2, 4, 5)),
@@ -493,7 +508,7 @@
             dma((2,)),
             dma((2,)),
             dma((3,)),
-            dma((3,)),
+            dma((2, 3)),
             dma((4,)),
             dma((4,)),
             pltpu.SemaphoreType.REGULAR,

time: 40.4 us -> 38.3 us (0.948)
  Pallas kernels: 39.7 us -> 37.6 us
    pallas_call x1, Pallas kernels: 39.7 us -> 37.6 us  [body(): pl.pallas_call(kernel, out_shape=pltpu.VMEM((4, 32), F32), in_specs=[hbm]...]
where the time goes in v3:
time: 38.3 us; the launch traced here: 38.2 us
  Pallas kernels  37.6 us (98%)
  local copies, waits for them, and re-layouts  0.58 us (2%)
    pallas_call x1, Pallas kernels, body(): pl.pallas_call(kernel, out_shape=pltpu.VMEM((4, 32), F32), in_specs=[hbm]...  37.6 us

profile of v3, /device:TPU:1, one launch (start us, length us, event | category | flops | bytes accessed | tf_op | source)
XLA Modules:
  0.0 38.2 jit_solution(9616891883408672999)
XLA Ops:
  0.0 37.6 %xxt.1 = f32[4,32]{1,0:T(4,128)S(1)} custom-call(bf16[4,32]{1,0:T(4,128)(2,1)} %rhs_hbm.1, s32[9]{0:T(128)} %sizes_hbm.1, bf16[32,29400]{1,0:T(8,128)(2,1)} %xsep_ref.1, bf16[32,4096]{1,0:T(8,128)(2,1)} %xloc_ref.1), custom_call_target="tpu_custom_call" | custom-call | tf_op jit(solution)/shard_map/xxt/pallas_call | solution.py:479
  37.6 0.6 %copy.6 = f32[4,32]{1,0:T(4,128)} copy(f32[4,32]{1,0:T(4,128)S(1)} %xxt.1) | data formatting | bytes 1024

commit v4 on v3

--- a/solution.py
+++ b/solution.py
@@ -16,6 +16,8 @@
 WIDE = (13, 7, 8, 3)
 AT = (0, 13, 20, 28)
 BLOCKS = 31
+BEGIN = (0, 50, 75, 107)
+TILES = 116
 KEEP = ((0, 12800), (12800, 19200), (19200, 27200), (27200, 29400))
 COLS = 29400
 ENDS = (12800, 19200, 22400, 25600, 27200, 28000, 28800, 29200, 29400)
@@ -87,73 +89,97 @@
     def drain(ref, sem):
         pltpu.make_async_copy(ref, ref, sem).wait()
 
+    base = me - me % Z1 + core - y1 * Y1 - y0 * Y0
+
+    def place(kk):
+        return (kk // 2) * X0 + (kk % 2) * Z0
+
+    def owner_a(a):
+        return base + (a % 2) * Y1 + core * Y0 + place(a // 2)
+
+    def owner_b(b):
+        return base + y1 * Y1 + (1 - core) * Y0 + place(b)
+
+    def owner_c(d):
+        return base + y1 * Y1 + y0 * Y0 + (core - z1) * Z1 + place(d)
+
+    role_a = y0 == core
+    a_mine = 2 * k + y1
+    owns_a = jnp.logical_and(role_a, a_mine < WIDE[0])
+    owns_b = jnp.logical_and(jnp.logical_not(role_a), k < WIDE[1])
+    slot_a = 16 * y1 + 8 * y0 + k
+    slot_b = 8 * y0 + k
+    slot_c = 8 * z1 + k
+    owns_c = z1 == core
+    owns_ab = jnp.logical_or(owns_a, owns_b)
+
     depth = (me // Z1) % 8
 
     def along(step):
         return me + ((depth + step + 8) % 8 - depth) * Z1
 
     barrier = pltpu.get_barrier_semaphore()
-    greeted = [partner(m) for m in PLANE + [m | Z1 for m in LINE]]
-    greeted += [along(s) for s in (2, -2, 1, -1)] + [partner(CORE)]
-    for device in greeted:
-        pl.semaphore_signal(barrier, inc=1, device_id=(device,), device_id_type=MESH)
+
+    def greet(devices):
+        for device in devices:
+            pl.semaphore_signal(barrier, inc=1, device_id=(device,), device_id_type=MESH)
+
+    def count(flag):
+        return flag.astype(jnp.int32)
+
+    @pl.when(owns_a)
+    def _():
+        greet(partner(m) for m in PLANE)
+
+    @pl.when(owns_b)
+    def _():
+        greet(partner(m) for m in PAIR)
+
+    @pl.when(owns_c)
+    def _():
+        greet(partner(m) for m in SLAB)
+
+    @pl.when(jnp.logical_not(owns_ab))
+    def _():
+        greet(partner(m) for m in LINE)
+
+    greet([along(s) for s in (2, -2, 1, -1)] + [partner(CORE)])
+    line_owners = 7 - count(role_a) * y1
+    greetings = (
+        (WIDE[0] - count(owns_a)) + (WIDE[1] - count(owns_b)) + (WIDE[2] - count(owns_c))
+        + (8 - line_owners - (1 - count(owns_ab))) + 5
+    )
 
     rhs_copy = pltpu.make_async_copy(rhs_hbm, rhs_ref, small_sem.at[0])
     sizes_copy = pltpu.make_async_copy(sizes_hbm, sizes_ref, small_sem.at[1])
     rhs_copy.start()
     sizes_copy.start()
 
-    loads = {}
-    for zone in range(4):
-        for half in (1, 0):
-            owner = core if half == 0 else 1 - core
-            group = []
-            for s in range(4):
-                begin0, begin1 = window(zone, s), window(zone, 4 + s)
-                width = WIDE[zone] * 128
-                at = AT[zone] * 128
-                rows = pl.ds(32 * s, 32)
-                sem = load_sem.at[half, zone, s]
-                if zone == 3 and s == 3:
-                    group.append((begin0, begin1, sem, rows, at, owner))
-                    continue
-                start = pl.multiple_of((begin0 + owner * (begin1 - begin0)) * 128, 128)
-                copy = pltpu.make_async_copy(
-                    xsep_ref.at[:, pl.ds(start, width)], xs.at[half, rows, pl.ds(at, width)], sem
-                )
-                copy.start()
-                group.append(copy)
-            loads[zone, half] = group
-
-    def last_copies(half, last):
-        begin0, begin1, sem, rows, at, owner = loads[3, half][3]
-        if not last:
-            return [pltpu.make_async_copy(
-                xsep_ref.at[:, pl.ds(begin0 * 128, 384)], xs.at[half, rows, pl.ds(at, 384)], sem)]
-        rest = COLS - (begin1 + 2) * 128
-        return [
-            pltpu.make_async_copy(
-                xsep_ref.at[:, pl.ds(begin1 * 128, 256)], xs.at[half, rows, pl.ds(at, 256)], sem),
-            pltpu.make_async_copy(
-                xsep_ref.at[:, pl.ds((begin1 + 2) * 128, rest)], tail, load_sem.at[half, 3, 4]),
-        ]
-
-    def last_do(action):
-        for half in (0, 1):
-            owner = core if half == 0 else 1 - core
-            for last in (False, True):
-                @pl.when(owner == int(last))
-                def _():
-                    for copy in last_copies(half, last):
-                        action(copy)
-
-    last_do(lambda copy: copy.start())
-    loc_copies = [
-        pltpu.make_async_copy(xloc_ref.at[:, pl.ds(1024 * s, 1024)], xl.at[pl.ds(32 * s, 32), :], loc_sem.at[s])
-        for s in range(4)
-    ]
-    for copy in loc_copies:
-        copy.start()
+    def load(zone, half, width):
+        first, tiles = ZONES[zone]
+        owner = core if half == 0 else 1 - core
+        start = pl.multiple_of((first + owner * (tiles // 2)) * 128, 128)
+        return pltpu.make_async_copy(
+            xsep_ref.at[:, pl.ds(start, width)], xs.at[half, :, pl.ds(BEGIN[zone] * 128, width)],
+            load_sem.at[half, zone])
+
+    def load_last(half, action):
+        @pl.when((core if half == 0 else 1 - core) == 0)
+        def _():
+            action(load(3, half, 9 * 128))
+
+        @pl.when((core if half == 0 else 1 - core) == 1)
+        def _():
+            action(load(3, half, 8 * 128))
+            action(pltpu.make_async_copy(
+                xsep_ref.at[:, pl.ds(COLS - COLS % 128, COLS % 128)], tail, load_sem.at[half, 4]))
+
+    for half in (1, 0):
+        for zone in range(3):
+            load(zone, half, ZONES[zone][1] * 64).start()
+        load_last(half, lambda copy: copy.start())
+    loc_copy = pltpu.make_async_copy(xloc_ref, xl, loc_sem)
+    loc_copy.start()
 
     row = lax.broadcasted_iota(jnp.int32, (16, 128), 0)
     lane = lax.broadcasted_iota(jnp.int32, (16, 128), 1)
@@ -166,9 +192,15 @@
     wide = jnp.dot(tall, pick_lanes.astype(BF16), preferred_element_type=F32)
     rhs16 = jnp.where(diagonal, wide, 0.0).astype(BF16)
 
+    def windows(zone, half):
+        found = []
+        for s in range(4):
+            at = (BEGIN[zone] + window(zone, s) - ZONES[zone][0]) * 128
+            found.append(xs[half, :, at : at + WIDE[zone] * 128])
+        return jnp.concatenate(found, axis=0)
+
     def contributions(zone, half, store):
-        columns = pl.ds(AT[zone] * 128, WIDE[zone] * 128)
-        product = jnp.dot(rhs16, xs[half, :, columns], preferred_element_type=F32)
+        product = jnp.dot(rhs16, windows(zone, half), preferred_element_type=F32)
         for j in range(WIDE[zone]):
             store[AT[zone] + j] = product[:, 128 * j : 128 * j + 128]
 
@@ -176,21 +208,19 @@
         @pl.when((core if half == 0 else 1 - core) == 1)
         def _():
             rest = jnp.concatenate([tail[...], jnp.zeros((32, 128 - tail.shape[1]), BF16)], axis=1)
-            xs[half, 96:128, BLOCKS * 128 - 128 : BLOCKS * 128] = rest
-
-    for zone in range(4):
-        for half in (1, 0):
-            for copy in loads[zone, half]:
-                if not isinstance(copy, tuple):
-                    copy.wait()
-        if zone == 3:
-            last_do(lambda copy: copy.wait())
-            place_tail(1)
-            place_tail(0)
-        contributions(zone, 1, send_core)
-        contributions(zone, 0, mine)
-
-    pl.semaphore_wait(barrier, len(greeted))
+            xs[half, :, TILES * 128 - 128 : TILES * 128] = rest
+
+    def contribute(half, store):
+        for zone in range(3):
+            load(zone, half, ZONES[zone][1] * 64).wait()
+            contributions(zone, half, store)
+        load_last(half, lambda copy: copy.wait())
+        place_tail(half)
+        contributions(3, half, store)
+
+    contribute(1, send_core)
+
+    pl.semaphore_wait(barrier, greetings)
     for step in (2, -2):
         pl.semaphore_signal(token, inc=1, device_id=(along(step),), device_id_type=MESH)
 
@@ -201,29 +231,7 @@
         copy = remote(send_core.at[blocks], recv_core.at[blocks], core_send.at[zone], core_recv.at[zone], sibling)
         copy.start()
         core_copies.append(copy)
-
-    base = me - me % Z1 + core - y1 * Y1 - y0 * Y0
-
-    def place(kk):
-        return (kk // 2) * X0 + (kk % 2) * Z0
-
-    def owner_a(a):
-        return base + (a % 2) * Y1 + core * Y0 + place(a // 2)
-
-    def owner_b(b):
-        return base + y1 * Y1 + (1 - core) * Y0 + place(b)
-
-    def owner_c(d):
-        return base + y1 * Y1 + y0 * Y0 + (core - z1) * Z1 + place(d)
-
-    role_a = y0 == core
-    a_mine = 2 * k + y1
-    owns_a = jnp.logical_and(role_a, a_mine < WIDE[0])
-    owns_b = jnp.logical_and(jnp.logical_not(role_a), k < WIDE[1])
-    slot_a = 16 * y1 + 8 * y0 + k
-    slot_b = 8 * y0 + k
-    slot_c = 8 * z1 + k
-    owns_c = z1 == core
+    contribute(0, mine)
 
     def scatter(zone, count, owner, slot, landing, sem):
         for j in range(count):
@@ -285,7 +293,6 @@
         drain(recv_ab.at[pl.ds(0, 15)], rs_recv.at[1])
         part_ab[...] = total(recv_ab, 16)
 
-    owns_ab = jnp.logical_or(owns_a, owns_b)
 
     @pl.when(owns_ab)
     def _():
@@ -344,16 +351,15 @@
 
     relay(3, 3).start()
 
-    for copy in loc_copies:
-        copy.wait()
-    interior = jnp.dot(rhs16, xl[...], preferred_element_type=F32).astype(BF16)
+    loc_copy.wait()
+    x_loc = jnp.concatenate([xl[:, 1024 * s : 1024 * s + 1024] for s in range(4)], axis=0)
+    interior = jnp.dot(rhs16, x_loc, preferred_element_type=F32).astype(BF16)
     contract = (((1,), (1,)), ((), ()))
-    acc = lax.dot_general(interior, xl[...], contract, preferred_element_type=F32)
+    acc = lax.dot_general(interior, x_loc, contract, preferred_element_type=F32)
 
     def product(zone, half):
         blocks = jnp.concatenate([full[half, AT[zone] + j] for j in range(WIDE[zone])], axis=1)
-        columns = pl.ds(AT[zone] * 128, WIDE[zone] * 128)
-        return lax.dot_general(blocks, xs[half, :, columns], contract, preferred_element_type=F32)
+        return lax.dot_general(blocks, windows(zone, half), contract, preferred_element_type=F32)
 
     def deep_total(part, landing):
         value = part[...]
@@ -444,18 +450,14 @@
         def _():
             drain(full.at[0, pl.ds(AT[zone], WIDE[zone])], ag_recv.at[0, zone])
 
-    drain_gather(owns_b, 1)
-    acc = acc + product(1, 0)
-    drain(full.at[1, pl.ds(AT[1], WIDE[1])], ag_recv.at[1, 1])
-    acc = acc + product(1, 1)
-    drain_gather(owns_c, 2)
-    acc = acc + product(2, 0)
-    drain(full.at[1, pl.ds(AT[2], WIDE[2])], ag_recv.at[1, 2])
-    acc = acc + product(2, 1)
-    drain_gather(owns_a, 0)
-    acc = acc + product(0, 0)
-    drain(full.at[1, pl.ds(AT[0], WIDE[0])], ag_recv.at[1, 0])
-    acc = acc + product(0, 1)
+    def arrived(owns, zone):
+        drain_gather(owns, zone)
+        drain(full.at[1, pl.ds(AT[zone], WIDE[zone])], ag_recv.at[1, zone])
+        return product(zone, 0) + product(zone, 1)
+
+    acc = acc + arrived(owns_b, 1)
+    acc = acc + arrived(owns_c, 2)
+    acc = acc + arrived(owns_a, 0)
     out_ref[...] = (acc[0:4, 0:32] + acc[4:8, 32:64]) + (acc[8:12, 64:96] + acc[12:16, 96:128])
 
     @pl.when(owns_a)
@@ -484,9 +486,9 @@
         scratch_shapes=[
             pltpu.VMEM((4, 32), BF16),
             pltpu.SMEM((9,), jnp.int32),
-            pltpu.VMEM((2, 128, BLOCKS * 128), BF16),
+            pltpu.VMEM((2, 32, TILES * 128), BF16),
             pltpu.VMEM((32, COLS % 128), BF16),
-            pltpu.VMEM((128, LOC // 4), BF16),
+            pltpu.VMEM((32, LOC), BF16),
             blocks((BLOCKS, 16, 128)),
             blocks((BLOCKS, 16, 128)),
             blocks((BLOCKS, 16, 128)),
@@ -499,8 +501,8 @@
             blocks((3, 16, 128)),
             pltpu.VMEM((2, BLOCKS, 16, 128), BF16),
             dma((2,)),
-            dma((2, 4, 5)),
-            dma((4,)),
+            dma((2, 5)),
+            dma,
             dma((4,)),
             dma((4,)),
             dma((10,)),

time: 38.3 us -> 37.7 us (0.984)
  Pallas kernels: 37.6 us -> 37 us
    pallas_call x1, Pallas kernels: 37.6 us -> 37 us  [body(): pl.pallas_call(kernel, out_shape=pltpu.VMEM((4, 32), F32), in_specs=[hbm]...]
where the time goes in v4:
time: 37.7 us; the launch traced here: 37.6 us
  Pallas kernels  37 us (98%)
  local copies, waits for them, and re-layouts  0.58 us (2%)
    pallas_call x1, Pallas kernels, body(): pl.pallas_call(kernel, out_shape=pltpu.VMEM((4, 32), F32), in_specs=[hbm]...  37 us

profile of v4, /device:TPU:1, one launch (start us, length us, event | category | flops | bytes accessed | tf_op | source)
XLA Modules:
  0.0 37.6 jit_solution(14158471971954284202)
XLA Ops:
  0.0 37.0 %xxt.1 = f32[4,32]{1,0:T(4,128)S(1)} custom-call(bf16[4,32]{1,0:T(4,128)(2,1)} %rhs_hbm.1, s32[9]{0:T(128)} %sizes_hbm.1, bf16[32,29400]{1,0:T(8,128)(2,1)} %xsep_ref.1, bf16[32,4096]{1,0:T(8,128)(2,1)} %xloc_ref.1), custom_call_target="tpu_custom_call" | custom-call | tf_op jit(solution)/shard_map/xxt/pallas_call | solution.py:481
  37.0 0.6 %copy.6 = f32[4,32]{1,0:T(4,128)} copy(f32[4,32]{1,0:T(4,128)S(1)} %xxt.1) | data formatting | bytes 1024

commit v5 on v4

--- a/solution.py
+++ b/solution.py
@@ -63,16 +63,17 @@
 def kernel(rhs_hbm, sizes_hbm, xsep_ref, xloc_ref, out_ref,
            rhs_ref, sizes_ref, xs, tail, xl, mine, send_core, recv_core, recv_ab, recv_c, recv_d, part_ab, part_c, deep_ab, deep_c, full,
            small_sem, load_sem, loc_sem, core_send, core_recv, rs_send, rs_recv, z_send, z_recv, ag_send, ag_recv,
-           relay_send, relay_recv, token):
+           relay_send, relay_recv, token, near):
     me = lax.axis_index("leaf")
 
     def bit(b):
-        return (me // b) % 2
+        return lax.rem(lax.div(me, jnp.int32(b)), jnp.int32(2))
 
     core = bit(CORE)
     y0, y1, z1 = bit(Y0), bit(Y1), bit(Z1)
-    k = 2 * ((me // X0) % 4) + bit(Z0)
-    delta = {b: (1 - 2 * bit(b)) * b for b in (CORE, X0, X1, Z0, Z1, Z2, Z3, Y0, Y1)}
+    k = 4 * bit(X1) + 2 * bit(X0) + bit(Z0)
+    turn = {b: 1 - 2 * bit(b) for b in (CORE, X0, X1, Z0, Z1, Z2, Z3, Y0, Y1)}
+    delta = {b: turn[b] * b for b in turn}
 
     def partner(mask):
         other = me
@@ -88,20 +89,6 @@
 
     def drain(ref, sem):
         pltpu.make_async_copy(ref, ref, sem).wait()
-
-    base = me - me % Z1 + core - y1 * Y1 - y0 * Y0
-
-    def place(kk):
-        return (kk // 2) * X0 + (kk % 2) * Z0
-
-    def owner_a(a):
-        return base + (a % 2) * Y1 + core * Y0 + place(a // 2)
-
-    def owner_b(b):
-        return base + y1 * Y1 + (1 - core) * Y0 + place(b)
-
-    def owner_c(d):
-        return base + y1 * Y1 + y0 * Y0 + (core - z1) * Z1 + place(d)
 
     role_a = y0 == core
     a_mine = 2 * k + y1
@@ -113,20 +100,25 @@
     owns_c = z1 == core
     owns_ab = jnp.logical_or(owns_a, owns_b)
 
-    depth = (me // Z1) % 8
+    depth = lax.rem(lax.div(me, jnp.int32(Z1)), jnp.int32(8))
 
     def along(step):
-        return me + ((depth + step + 8) % 8 - depth) * Z1
+        return me + (lax.rem(depth + (step + 8), jnp.int32(8)) - depth) * Z1
 
     barrier = pltpu.get_barrier_semaphore()
+    sibling = partner(CORE)
 
     def greet(devices):
         for device in devices:
-            pl.semaphore_signal(barrier, inc=1, device_id=(device,), device_id_type=MESH)
+            pl.semaphore_signal(barrier, inc=1, device_id=(device - core,), device_id_type=MESH)
 
     def count(flag):
         return flag.astype(jnp.int32)
 
+    @pl.when(core == 0)
+    def _():
+        pl.semaphore_signal(barrier, inc=1, device_id=(sibling,), device_id_type=MESH)
+
     @pl.when(owns_a)
     def _():
         greet(partner(m) for m in PLANE)
@@ -143,12 +135,16 @@
     def _():
         greet(partner(m) for m in LINE)
 
-    greet([along(s) for s in (2, -2, 1, -1)] + [partner(CORE)])
-    line_owners = 7 - count(role_a) * y1
-    greetings = (
-        (WIDE[0] - count(owns_a)) + (WIDE[1] - count(owns_b)) + (WIDE[2] - count(owns_c))
-        + (8 - line_owners - (1 - count(owns_ab))) + 5
-    )
+    greet(along(s) for s in (2, -2, 1, -1))
+    greetings = 0
+    for c in (0, 1):
+        takes_a = count(y0 == c)
+        has_a = takes_a * count(a_mine < WIDE[0])
+        has_b = (1 - takes_a) * count(k < WIDE[1])
+        line_owners = 7 - takes_a * y1
+        greetings += (
+            (WIDE[0] - has_a) + (WIDE[1] - has_b) + (WIDE[2] - count(z1 == c)) + (8 - line_owners - (1 - has_a - has_b)) + 4
+        )
 
     rhs_copy = pltpu.make_async_copy(rhs_hbm, rhs_ref, small_sem.at[0])
     sizes_copy = pltpu.make_async_copy(sizes_hbm, sizes_ref, small_sem.at[1])
@@ -180,6 +176,11 @@
         load_last(half, lambda copy: copy.start())
     loc_copy = pltpu.make_async_copy(xloc_ref, xl, loc_sem)
     loc_copy.start()
+
+    @pl.when(core == 1)
+    def _():
+        pl.semaphore_wait(barrier, 1)
+        pl.semaphore_signal(near, inc=1, device_id=(sibling,), device_id_type=MESH)
 
     row = lax.broadcasted_iota(jnp.int32, (16, 128), 0)
     lane = lax.broadcasted_iota(jnp.int32, (16, 128), 1)
@@ -220,11 +221,10 @@
 
     contribute(1, send_core)
 
-    pl.semaphore_wait(barrier, greetings)
-    for step in (2, -2):
-        pl.semaphore_signal(token, inc=1, device_id=(along(step),), device_id_type=MESH)
-
-    sibling = partner(CORE)
+    @pl.when(core == 0)
+    def _():
+        pl.semaphore_wait(near, 1)
+
     core_copies = []
     for zone in range(4):
         blocks = pl.ds(AT[zone], WIDE[zone])
@@ -233,30 +233,60 @@
         core_copies.append(copy)
     contribute(0, mine)
 
-    def scatter(zone, count, owner, slot, landing, sem):
-        for j in range(count):
-            block = AT[zone] + j
-            to = owner(j)
-
-            @pl.when(to == me)
+    @pl.when(core == 0)
+    def _():
+        pl.semaphore_wait(barrier, greetings)
+        pl.semaphore_signal(near, inc=1, device_id=(sibling,), device_id_type=MESH)
+
+    @pl.when(core == 1)
+    def _():
+        pl.semaphore_wait(near, 1)
+
+    for step in (2, -2):
+        pl.semaphore_signal(token, inc=1, device_id=(along(step),), device_id_type=MESH)
+
+    def place(mask):
+        return k + sum(turn[b] * w for b, w in ((X1, 4), (X0, 2), (Z0, 1)) if mask & b)
+
+    def scatter(zone, masks, ahead, item, slot, landing):
+        for mask in masks:
+            to = partner(mask) + ahead
+            j = item(mask)
+            wanted = j < WIDE[zone]
+
+            @pl.when(wanted if mask else jnp.logical_and(wanted, ahead != 0))
             def _():
-                landing[slot] = mine[block]
-
-            @pl.when(to != me)
-            def _():
-                remote(mine.at[block], landing.at[slot], rs_send.at[sem], rs_recv.at[sem], to).start()
+                remote(mine.at[AT[zone] + j], landing.at[slot], rs_send.at[zone], rs_recv.at[zone], to).start()
+
+    def scatter_a():
+        scatter(0, masks_of((X0, X1, Z0, Y1)) + [0], (core - y0) * Y0,
+                lambda m: 2 * place(m) + (y1 + turn[Y1] if m & Y1 else y1), slot_a, recv_ab)
+
+        @pl.when(owns_a)
+        def _():
+            recv_ab[slot_a] = mine[a_mine]
+
+    def scatter_b():
+        scatter(1, LINE + [0], (1 - core - y0) * Y0, place, slot_b, recv_ab)
+
+        @pl.when(owns_b)
+        def _():
+            recv_ab[slot_b] = mine[AT[1] + k]
+
+    def scatter_c():
+        scatter(2, LINE + [0], (core - z1) * Z1, place, slot_c, recv_c)
+
+        @pl.when(owns_c)
+        def _():
+            recv_c[slot_c] = mine[AT[2] + k]
 
     for zone in range(4):
         core_copies[zone].wait_recv()
         for j in range(WIDE[zone]):
             block = AT[zone] + j
             mine[block] = mine[block] + recv_core[block]
-        if zone == 0:
-            scatter(0, WIDE[0], owner_a, slot_a, recv_ab, 0)
-        elif zone == 1:
-            scatter(1, WIDE[1], owner_b, slot_b, recv_ab, 1)
-        elif zone == 2:
-            scatter(2, WIDE[2], owner_c, slot_c, recv_c, 2)
+        if zone < 3:
+            (scatter_a, scatter_b, scatter_c)[zone]()
 
     def d_copy(n, mask):
         return remote(mine.at[pl.ds(AT[3], WIDE[3])], recv_d.at[n], rs_send.at[3 + n], rs_recv.at[3 + n], partner(mask))
@@ -514,6 +544,7 @@
             dma((4,)),
             dma((4,)),
             pltpu.SemaphoreType.REGULAR,
+            pltpu.SemaphoreType.REGULAR,
         ],
         compiler_params=pltpu.CompilerParams(
             collective_id=0, has_side_effects=True, vmem_limit_bytes=60 * 1024 * 1024

time: 37.7 us -> 36.4 us (0.966)
  Pallas kernels: 37 us -> 35.7 us
    pallas_call x1, Pallas kernels: 37 us -> 35.7 us  [body(): pl.pallas_call(kernel, out_shape=pltpu.VMEM((4, 32), F32), in_specs=[hbm]...]
where the time goes in v5:
time: 36.4 us; the launch traced here: 36.3 us
  Pallas kernels  35.7 us (98%)
  local copies, waits for them, and re-layouts  0.58 us (2%)
    pallas_call x1, Pallas kernels, body(): pl.pallas_call(kernel, out_shape=pltpu.VMEM((4, 32), F32), in_specs=[hbm]...  35.7 us

profile of v5, /device:TPU:1, one launch (start us, length us, event | category | flops | bytes accessed | tf_op | source)
XLA Modules:
  0.0 36.3 jit_solution(6246328135113153856)
XLA Ops:
  0.0 35.7 %xxt.1 = f32[4,32]{1,0:T(4,128)S(1)} custom-call(bf16[4,32]{1,0:T(4,128)(2,1)} %rhs_hbm.1, s32[9]{0:T(128)} %sizes_hbm.1, bf16[32,29400]{1,0:T(8,128)(2,1)} %xsep_ref.1, bf16[32,4096]{1,0:T(8,128)(2,1)} %xloc_ref.1), custom_call_target="tpu_custom_call" | custom-call | tf_op jit(solution)/shard_map/xxt/pallas_call | solution.py:511
  35.7 0.6 %copy.6 = f32[4,32]{1,0:T(4,128)} copy(f32[4,32]{1,0:T(4,128)S(1)} %xxt.1) | data formatting | bytes 1024

commit v6 on v5

--- a/solution.py
+++ b/solution.py
@@ -211,15 +211,13 @@
             rest = jnp.concatenate([tail[...], jnp.zeros((32, 128 - tail.shape[1]), BF16)], axis=1)
             xs[half, :, TILES * 128 - 128 : TILES * 128] = rest
 
-    def contribute(half, store):
-        for zone in range(3):
+    def contribute(zone, half, store):
+        if zone < 3:
             load(zone, half, ZONES[zone][1] * 64).wait()
-            contributions(zone, half, store)
-        load_last(half, lambda copy: copy.wait())
-        place_tail(half)
-        contributions(3, half, store)
-
-    contribute(1, send_core)
+        else:
+            load_last(half, lambda copy: copy.wait())
+            place_tail(half)
+        contributions(zone, half, store)
 
     @pl.when(core == 0)
     def _():
@@ -227,11 +225,13 @@
 
     core_copies = []
     for zone in range(4):
+        contribute(zone, 1, send_core)
         blocks = pl.ds(AT[zone], WIDE[zone])
         copy = remote(send_core.at[blocks], recv_core.at[blocks], core_send.at[zone], core_recv.at[zone], sibling)
         copy.start()
         core_copies.append(copy)
-    contribute(0, mine)
+    for zone in range(4):
+        contribute(zone, 0, mine)
 
     @pl.when(core == 0)
     def _():
@@ -486,8 +486,8 @@
         return product(zone, 0) + product(zone, 1)
 
     acc = acc + arrived(owns_b, 1)
+    acc = acc + arrived(owns_a, 0)
     acc = acc + arrived(owns_c, 2)
-    acc = acc + arrived(owns_a, 0)
     out_ref[...] = (acc[0:4, 0:32] + acc[4:8, 32:64]) + (acc[8:12, 64:96] + acc[12:16, 96:128])
 
     @pl.when(owns_a)

time: 36.4 us -> 36.2 us (level)
  no operation moved by 1% of the time
where the time goes in v6:
time: 36.2 us; the launch traced here: 36.1 us
  Pallas kernels  35.5 us (98%)
  local copies, waits for them, and re-layouts  0.58 us (2%)
    pallas_call x1, Pallas kernels, body(): pl.pallas_call(kernel, out_shape=pltpu.VMEM((4, 32), F32), in_specs=[hbm]...  35.5 us

profile of v6, /device:TPU:1, one launch (start us, length us, event | category | flops | bytes accessed | tf_op | source)
XLA Modules:
  0.0 36.1 jit_solution(13936029977827080103)
XLA Ops:
  0.0 35.5 %xxt.1 = f32[4,32]{1,0:T(4,128)S(1)} custom-call(bf16[4,32]{1,0:T(4,128)(2,1)} %rhs_hbm.1, s32[9]{0:T(128)} %sizes_hbm.1, bf16[32,29400]{1,0:T(8,128)(2,1)} %xsep_ref.1, bf16[32,4096]{1,0:T(8,128)(2,1)} %xloc_ref.1), custom_call_target="tpu_custom_call" | custom-call | tf_op jit(solution)/shard_map/xxt/pallas_call | solution.py:511
  35.5 0.6 %copy.6 = f32[4,32]{1,0:T(4,128)} copy(f32[4,32]{1,0:T(4,128)S(1)} %xxt.1) | data formatting | bytes 1024

commit v7 on v6

--- a/solution.py
+++ b/solution.py
@@ -55,9 +55,7 @@
 PLANE = masks_of((X0, X1, Z0, Y0, Y1))
 PAIR = masks_of((X0, X1, Z0, Y0))
 LINE = masks_of((X0, X1, Z0))
-SLAB = masks_of((X0, X1, Z0, Z1))
 DEPTH = [m * Z1 for m in (4, 5, 3, 6, 2, 7, 1)]
-DEPTH_C = [m * Z1 for m in (4, 2, 6)]
 
 
 def kernel(rhs_hbm, sizes_hbm, xsep_ref, xloc_ref, out_ref,
@@ -96,8 +94,6 @@
     owns_b = jnp.logical_and(jnp.logical_not(role_a), k < WIDE[1])
     slot_a = 16 * y1 + 8 * y0 + k
     slot_b = 8 * y0 + k
-    slot_c = 8 * z1 + k
-    owns_c = z1 == core
     owns_ab = jnp.logical_or(owns_a, owns_b)
 
     depth = lax.rem(lax.div(me, jnp.int32(Z1)), jnp.int32(8))
@@ -126,10 +122,6 @@
     @pl.when(owns_b)
     def _():
         greet(partner(m) for m in PAIR)
-
-    @pl.when(owns_c)
-    def _():
-        greet(partner(m) for m in SLAB)
 
     @pl.when(jnp.logical_not(owns_ab))
     def _():
@@ -143,7 +135,7 @@
         has_b = (1 - takes_a) * count(k < WIDE[1])
         line_owners = 7 - takes_a * y1
         greetings += (
-            (WIDE[0] - has_a) + (WIDE[1] - has_b) + (WIDE[2] - count(z1 == c)) + (8 - line_owners - (1 - has_a - has_b)) + 4
+            (WIDE[0] - has_a) + (WIDE[1] - has_b) + (8 - line_owners - (1 - has_a - has_b)) + 4
         )
 
     rhs_copy = pltpu.make_async_copy(rhs_hbm, rhs_ref, small_sem.at[0])
@@ -274,11 +266,8 @@
             recv_ab[slot_b] = mine[AT[1] + k]
 
     def scatter_c():
-        scatter(2, LINE + [0], (core - z1) * Z1, place, slot_c, recv_c)
-
-        @pl.when(owns_c)
-        def _():
-            recv_c[slot_c] = mine[AT[2] + k]
+        scatter(2, LINE, 0, place, k, recv_c)
+        recv_c[k] = mine[AT[2] + k]
 
     for zone in range(4):
         core_copies[zone].wait_recv()
@@ -329,21 +318,13 @@
         for copy in deep_copies(part_ab, deep_ab, 0):
             copy.start()
 
-    def c_far(action):
-        for m in DEPTH_C:
-            if m & Z3:
-                @pl.when(core == 0)
-                def _():
-                    action(m)
-            else:
-                action(m)
-
-    @pl.when(owns_c)
-    def _():
-        drain(recv_c.at[pl.ds(0, 15)], rs_recv.at[2])
-        part_c[...] = total(recv_c, 16)
-        c_far(lambda m: remote(
-            part_c, deep_c.at[m // Z2 - 1], z_send.at[1], z_recv.at[1], partner(m)).start())
+    drain(recv_c.at[pl.ds(0, 7)], rs_recv.at[2])
+    part_c[...] = total(recv_c, 8)
+    for m, copy in zip(DEPTH, deep_copies(part_c, deep_c, 1)):
+        if m & Z3:
+            pl.when(core == 0)(copy.start)
+        else:
+            copy.start()
 
     d_do(lambda copy: copy.start())
 
@@ -419,23 +400,21 @@
         full[0, AT[1] + k] = rounded(deep_total(part_ab, deep_ab), columns, end, 1)
         gather(AT[1] + k, PAIR, 1)
 
-    @pl.when(owns_c)
-    def _():
-        @pl.when(core == 0)
-        def _():
-            drain(deep_c, z_recv.at[1])
-
-        @pl.when(core == 1)
-        def _():
-            drain(deep_c.at[pl.ds(0, 1)], z_recv.at[1])
-
-        columns, end = column_of(2, core, k)
-        value = part_c[...]
-        for m in range(1, 4):
-            bound = ENDS[3] if m == 1 else jnp.where(core == 0, ENDS[2], 0)
-            value = value + jnp.where(columns < bound, deep_c[m - 1], 0.0)
-        full[0, AT[2] + k] = rounded(value, columns, end, 2)
-        gather(AT[2] + k, SLAB, 2)
+    @pl.when(core == 0)
+    def _():
+        drain(deep_c, z_recv.at[1])
+
+    @pl.when(core == 1)
+    def _():
+        drain(deep_c.at[pl.ds(0, 3)], z_recv.at[1])
+
+    columns, end = column_of(2, core, k)
+    value = part_c[...]
+    for m in range(1, 8):
+        bound = ENDS[4] if m == 1 else ENDS[3] if m < 4 else jnp.where(core == 0, ENDS[2], 0)
+        value = value + jnp.where(columns < bound, deep_c[m - 1], 0.0)
+    full[0, AT[2] + k] = rounded(value, columns, end, 2)
+    gather(AT[2] + k, LINE, 2)
 
     acc = acc + product(3, 0)
     relay(3, 3).wait_recv()
@@ -456,22 +435,26 @@
 
     drain_scatter(owns_a, 0)
     drain_scatter(owns_b, 1)
-    drain_scatter(owns_c, 2)
+    drain(mine.at[pl.ds(0, 7)], rs_send.at[2])
     d_do(lambda copy: copy.wait_send())
 
     @pl.when(owns_ab)
     def _():
         drain(deep_ab, z_send.at[0])
 
-    @pl.when(jnp.logical_and(owns_c, core == 0))
+    @pl.when(core == 0)
     def _():
         drain(deep_c, z_send.at[1])
 
-    @pl.when(jnp.logical_and(owns_c, core == 1))
-    def _():
-        drain(deep_c.at[pl.ds(0, 1)], z_send.at[1])
+    @pl.when(core == 1)
+    def _():
+        drain(deep_c.at[pl.ds(0, 3)], z_send.at[1])
 
     def drain_gather(owns, zone):
+        if owns is None:
+            drain(full.at[0, pl.ds(AT[zone], WIDE[zone] - 1)], ag_recv.at[0, zone])
+            return
+
         @pl.when(owns)
         def _():
             drain(full.at[0, pl.ds(AT[zone], WIDE[zone] - 1)], ag_recv.at[0, zone])
@@ -487,7 +470,7 @@
 
     acc = acc + arrived(owns_b, 1)
     acc = acc + arrived(owns_a, 0)
-    acc = acc + arrived(owns_c, 2)
+    acc = acc + arrived(None, 2)
     out_ref[...] = (acc[0:4, 0:32] + acc[4:8, 32:64]) + (acc[8:12, 64:96] + acc[12:16, 96:128])
 
     @pl.when(owns_a)
@@ -499,9 +482,7 @@
     def _():
         drain(full.at[0, pl.ds(0, 31)], ag_send.at[1])
 
-    @pl.when(owns_c)
-    def _():
-        drain(full.at[0, pl.ds(0, 31)], ag_send.at[2])
+    drain(full.at[0, pl.ds(0, 15)], ag_send.at[2])
 
 
 def body(rhs, x_sep, x_loc, sep_sizes):
@@ -523,12 +504,12 @@
             blocks((BLOCKS, 16, 128)),
             blocks((BLOCKS, 16, 128)),
             blocks((32, 16, 128)),
-            blocks((16, 16, 128)),
+            blocks((8, 16, 128)),
             blocks((7, WIDE[3], 16, 128)),
             blocks((16, 128)),
             blocks((16, 128)),
             blocks((7, 16, 128)),
-            blocks((3, 16, 128)),
+            blocks((7, 16, 128)),
             pltpu.VMEM((2, BLOCKS, 16, 128), BF16),
             dma((2,)),
             dma((2, 5)),

time: 36.2 us -> 36.2 us (level)
  no operation moved by 1% of the time
where the time goes in v7:
time: 36.2 us; the launch traced here: 36.1 us
  Pallas kernels  35.5 us (98%)
  local copies, waits for them, and re-layouts  0.58 us (2%)
    pallas_call x1, Pallas kernels, body(): pl.pallas_call(kernel, out_shape=pltpu.VMEM((4, 32), F32), in_specs=[hbm]...  35.5 us

profile of v7, /device:TPU:1, one launch (start us, length us, event | category | flops | bytes accessed | tf_op | source)
XLA Modules:
  0.0 36.1 jit_solution(5191511476888213237)
XLA Ops:
  0.0 35.5 %xxt.1 = f32[4,32]{1,0:T(4,128)S(1)} custom-call(bf16[4,32]{1,0:T(4,128)(2,1)} %rhs_hbm.1, s32[9]{0:T(128)} %sizes_hbm.1, bf16[32,29400]{1,0:T(8,128)(2,1)} %xsep_ref.1, bf16[32,4096]{1,0:T(8,128)(2,1)} %xloc_ref.1), custom_call_target="tpu_custom_call" | custom-call | tf_op jit(solution)/shard_map/xxt/pallas_call | solution.py:492
  35.5 0.6 %copy.6 = f32[4,32]{1,0:T(4,128)} copy(f32[4,32]{1,0:T(4,128)S(1)} %xxt.1) | data formatting | bytes 1024
